TPU v7x, 32 devices: a whole 2x2x4 slice. The times are simulated.
32 devices in a mesh: dp: 8 (over z, y), seq: 4 (over x, core).
Axes of the slice: x: 2, y: 2, z: 4, core: 2. Of those that a mesh axis runs over, the one named last changes fastest.
Arguments:
- inputs: bfloat16 [32, 1024, 512], P('dp', 'seq'), may hold values from -6 to 6
- memory: bfloat16 [32, 1024, 512], P('dp', 'seq'), may hold values from -6 to 6
- seg_ids: int32 [32, 1024], P('dp'), may hold values from 0 to 5, never falling along the last dimension, each value on 1 to 800 neighbouring positions
- mem_lengths: int32 [32, 6], P('dp'), may hold values from 1 to 512, 1024 in all within a row
- cotangent: bfloat16 [32, 1024, 512], P('dp', 'seq'), may hold values from -6 to 6
- qkv_weight: bfloat16 [512, 1536], P(('dp', 'seq')), may hold values from -0.25 to 0.25
- self_out_weight: bfloat16 [512, 512], P(('dp', 'seq')), may hold values from -1 to 1
- cross_q_weight: bfloat16 [512, 512], P(('dp', 'seq')), may hold values from -0.25 to 0.25
- cross_kv_weight: bfloat16 [512, 1024], P(('dp', 'seq')), may hold values from -0.25 to 0.25
- cross_out_weight: bfloat16 [512, 512], P(('dp', 'seq')), may hold values from -1 to 1
- ffn_in_weight: bfloat16 [512, 2048], P(('dp', 'seq')), may hold values from -0.25 to 0.25
- ffn_in_bias: bfloat16 [2048], P(('dp', 'seq')), may hold values from -3 to 3
- ffn_out_weight: bfloat16 [2048, 512], P(('dp', 'seq')), may hold values from -0.125 to 0.125
- norm_gains: bfloat16 [3, 512], P(None, ('dp', 'seq')), may hold values from 0.099609375 to 1.8984375
- shift_vectors: bfloat16 [4, 512], P(None, ('dp', 'seq')), may hold values from -3 to 3
Outputs:
- output: bfloat16 [32, 1024, 512], P('dp', 'seq')
- input_grad: float32 [32, 1024, 512], P('dp', 'seq')
- memory_grad: float32 [32, 1024, 512], P('dp', 'seq')
- qkv_grad: float32 [512, 1536], P(('dp', 'seq'))
- self_out_grad: float32 [512, 512], P(('dp', 'seq'))
- cross_q_grad: float32 [512, 512], P(('dp', 'seq'))
- cross_kv_grad: float32 [512, 1024], P(('dp', 'seq'))
- cross_out_grad: float32 [512, 512], P(('dp', 'seq'))
- ffn_in_grad: float32 [512, 2048], P(('dp', 'seq'))
- ffn_bias_grad: float32 [2048], P(('dp', 'seq'))
- ffn_out_grad: float32 [2048, 512], P(('dp', 'seq'))
- gains_grad: float32 [3, 512], P(None, ('dp', 'seq'))
- shifts_grad: float32 [4, 512], P(None, ('dp', 'seq'))
Inputs may be any that keep to these rules, and one draw needn't show every extreme that they name: `seg_ids`: sentence numbers never fall along a row and every number appears; in each row one sentence has exactly 800 tokens. `mem_lengths`: each row's lengths add up to 1024; sentence s reads the memory positions that follow those of sentences before it; the largest of a row is exactly 512.
All inputs are finite; a program needn't handle non-finite values.
Results may differ from a plain program's by a relative error of at most 0.02.
Values may be sent and summed in bfloat16 or wider, within the bound.
No kernel may reach another device: no remote copies, remote signals or barrier semaphores. Data moves between devices by JAX's collectives and lax.ppermute only.
A program may use at most 128 MiB of HBM per device.

v0:
```python
import jax
import jax.numpy as jnp
from jax import lax
from jax.sharding import PartitionSpec as P

HEAD = 64


def project(left_side, right_side):
    return jnp.dot(left_side, right_side, preferred_element_type=jnp.float32)


def project_back(left_side, right_side):
    return jnp.einsum("tj,ij->ti", left_side, right_side, preferred_element_type=jnp.float32)


def outer_sum(left_side, right_side):
    return jnp.einsum("ti,tj->ij", left_side, right_side, preferred_element_type=jnp.float32)


def norm_forward(values, gain_row, shift_row):
    row_mean = jnp.mean(values, axis=-1, keepdims=True)
    centered = values - row_mean
    inverse = lax.rsqrt(jnp.mean(centered * centered, axis=-1, keepdims=True) + 1e-05)
    normed = centered * inverse
    return (normed * gain_row + shift_row, normed, inverse)


def norm_backward(upstream, normed, inverse, gain_row):
    gain_part = jnp.sum(upstream * normed, axis=0)
    shift_part = jnp.sum(upstream, axis=0)
    scaled = upstream * gain_row
    centered = scaled - jnp.mean(scaled, axis=-1, keepdims=True)
    value_part = inverse * (centered - normed * jnp.mean(scaled * normed, axis=-1, keepdims=True))
    return (value_part, gain_part, shift_part)


def masked_scores(query_rows, key_rows, allowed):
    scores = jnp.einsum("qpe,kpe->pqk", query_rows, key_rows, preferred_element_type=jnp.float32)
    return jnp.where(allowed[None], scores * HEAD ** (-0.5), -1000000000.0)


def attend_forward(query_rows, key_rows, value_rows, allowed):
    scores = masked_scores(query_rows, key_rows, allowed)
    row_max = jnp.max(scores, axis=-1, keepdims=True)
    weights = jnp.exp(scores - row_max)
    row_total = jnp.sum(weights, axis=-1, keepdims=True)
    probs_low = (weights / row_total).astype(jnp.bfloat16)
    context = jnp.einsum("pqk,kpe->qpe", probs_low, value_rows, preferred_element_type=jnp.float32)
    return (context.astype(jnp.bfloat16), row_max + jnp.log(row_total))


def attend_backward(query_rows, key_rows, value_rows, allowed, log_total, d_context):
    probs = jnp.exp(masked_scores(query_rows, key_rows, allowed) - log_total)
    d_probs = jnp.einsum("qpe,kpe->pqk", d_context, value_rows, preferred_element_type=jnp.float32)
    d_value = jnp.einsum(
        "pqk,qpe->kpe", probs.astype(jnp.bfloat16), d_context, preferred_element_type=jnp.float32
    )
    row_delta = jnp.sum(probs * d_probs, axis=-1, keepdims=True)
    d_scores = (probs * (d_probs - row_delta) * HEAD ** (-0.5)).astype(jnp.bfloat16)
    d_query = jnp.einsum("pqk,kpe->qpe", d_scores, key_rows, preferred_element_type=jnp.float32)
    d_key = jnp.einsum("pqk,qpe->kpe", d_scores, query_rows, preferred_element_type=jnp.float32)
    return (d_query.astype(jnp.bfloat16), d_key.astype(jnp.bfloat16), d_value.astype(jnp.bfloat16))


def self_mask(segments):
    places = jnp.arange(segments.shape[0], dtype=jnp.int32)
    return (places[None, :] <= places[:, None]) & (segments[:, None] == segments[None, :])


def cross_mask(segments, mem_segments):
    return segments[:, None] == mem_segments[None, :]


def on_device(
    inputs,
    memory,
    seg_ids,
    mem_lengths,
    cotangent,
    qkv_weight,
    self_out_weight,
    cross_q_weight,
    cross_kv_weight,
    cross_out_weight,
    ffn_in_weight,
    ffn_in_bias,
    ffn_out_weight,
    norm_gains,
    shift_vectors,
):
    row_count, tok_span, model_width = inputs.shape
    mem_span = memory.shape[1]
    groups = lax.axis_size("seq")
    head_part = model_width // groups
    head_pairs = head_part // HEAD
    full_len = tok_span * groups
    mem_full = mem_span * groups
    gathered = (
        lax.all_gather(qkv_weight, ("dp", "seq"), axis=0, tiled=True),
        lax.all_gather(self_out_weight, ("dp", "seq"), axis=0, tiled=True),
        lax.all_gather(cross_q_weight, ("dp", "seq"), axis=0, tiled=True),
        lax.all_gather(cross_kv_weight, ("dp", "seq"), axis=0, tiled=True),
        lax.all_gather(cross_out_weight, ("dp", "seq"), axis=0, tiled=True),
        lax.all_gather(ffn_in_weight, ("dp", "seq"), axis=0, tiled=True),
        lax.all_gather(ffn_in_bias, ("dp", "seq"), axis=0, tiled=True),
        lax.all_gather(ffn_out_weight, ("dp", "seq"), axis=0, tiled=True),
        lax.all_gather(norm_gains, ("dp", "seq"), axis=1, tiled=True),
        lax.all_gather(shift_vectors, ("dp", "seq"), axis=1, tiled=True),
    )
    (
        self_qkv,
        self_proj,
        cross_query,
        cross_pair,
        cross_proj,
        ffn_up,
        ffn_bias,
        ffn_down,
        gain_low,
        shift_low,
    ) = gathered
    gain_rows = gain_low.astype(jnp.float32)
    shift_rows = shift_low.astype(jnp.float32)
    input_low = inputs.reshape(-1, model_width)
    input_full = input_low.astype(jnp.float32)
    memory_low = memory.reshape(-1, model_width)
    qkv_low = (
        project(input_low, self_qkv)
        .astype(jnp.bfloat16)
        .reshape(row_count, tok_span, 3, model_width)
    )
    qkv_heads = lax.all_to_all(qkv_low, "seq", split_axis=3, concat_axis=1, tiled=True)
    qkv_split = qkv_heads.reshape(row_count, full_len, 3, head_pairs, HEAD)

    def self_forward(packed):
        qkv_row, segments = packed
        return attend_forward(qkv_row[:, 0], qkv_row[:, 1], qkv_row[:, 2], self_mask(segments))

    self_ctx, self_lse = lax.map(self_forward, (qkv_split, seg_ids))
    ctx_tokens = lax.all_to_all(
        self_ctx.reshape(row_count, full_len, head_part),
        "seq",
        split_axis=1,
        concat_axis=2,
        tiled=True,
    )
    ctx_low = ctx_tokens.reshape(-1, model_width)
    attn_out = project(ctx_low, self_proj)
    first, normed_one, inverse_one = norm_forward(
        input_full + attn_out, gain_rows[0], shift_rows[0]
    )
    first_low = first.astype(jnp.bfloat16)
    query_low = (
        project(first_low, cross_query)
        .astype(jnp.bfloat16)
        .reshape(row_count, tok_span, 1, model_width)
    )
    pair_low = (
        project(memory_low, cross_pair)
        .astype(jnp.bfloat16)
        .reshape(row_count, mem_span, 2, model_width)
    )
    cross_in = (
        lax.all_to_all(query_low, "seq", split_axis=3, concat_axis=1, tiled=True),
        lax.all_to_all(pair_low, "seq", split_axis=3, concat_axis=1, tiled=True),
    )
    query_heads = cross_in[0].reshape(row_count, full_len, head_pairs, HEAD)
    pair_heads = cross_in[1].reshape(row_count, mem_full, 2, head_pairs, HEAD)
    ends = jnp.cumsum(mem_lengths, axis=1)
    mem_places = jnp.arange(mem_full, dtype=jnp.int32)
    mem_segments = jnp.sum(
        (mem_places[None, :, None] >= ends[:, None, :]).astype(jnp.int32), axis=2
    )

    def cross_forward(packed):
        query_row, pair_row, segments, mem_row = packed
        return attend_forward(
            query_row, pair_row[:, 0], pair_row[:, 1], cross_mask(segments, mem_row)
        )

    cross_ctx, cross_lse = lax.map(cross_forward, (query_heads, pair_heads, seg_ids, mem_segments))
    cross_tokens = lax.all_to_all(
        cross_ctx.reshape(row_count, full_len, head_part),
        "seq",
        split_axis=1,
        concat_axis=2,
        tiled=True,
    )
    cross_low = cross_tokens.reshape(-1, model_width)
    cross_out = project(cross_low, cross_proj)
    second, normed_two, inverse_two = norm_forward(first + cross_out, gain_rows[1], shift_rows[1])
    second_low = second.astype(jnp.bfloat16)
    pre_act = project(second_low, ffn_up) + ffn_bias.astype(jnp.float32)
    hidden, gelu_pull = jax.vjp(jax.nn.gelu, pre_act)
    hidden_low = hidden.astype(jnp.bfloat16)
    ffn_out = project(hidden_low, ffn_down) + shift_rows[3]
    result, normed_three, inverse_three = norm_forward(
        second + ffn_out + input_full, gain_rows[2], shift_rows[2]
    )
    output = result.astype(jnp.bfloat16).reshape(row_count, tok_span, model_width)
    upstream = cotangent.reshape(-1, model_width).astype(jnp.float32)
    d_three, gain_three, shift_three = norm_backward(
        upstream, normed_three, inverse_three, gain_rows[2]
    )
    d_ffn = d_three.astype(jnp.bfloat16)
    d_down = outer_sum(hidden_low, d_ffn)
    d_hidden = project_back(d_ffn, ffn_down)
    d_pre = gelu_pull(d_hidden)[0].astype(jnp.bfloat16)
    d_up = outer_sum(second_low, d_pre)
    d_bias = jnp.sum(d_pre.astype(jnp.float32), axis=0)
    ffn_shift = jnp.sum(d_three, axis=0)
    d_second = d_three + project_back(d_pre, ffn_up)
    d_two, gain_two, shift_two = norm_backward(d_second, normed_two, inverse_two, gain_rows[1])
    d_cross = d_two.astype(jnp.bfloat16)
    d_cross_proj = outer_sum(cross_low, d_cross)
    d_cross_ctx = (
        project_back(d_cross, cross_proj)
        .astype(jnp.bfloat16)
        .reshape(row_count, tok_span, model_width)
    )
    d_cross_heads = lax.all_to_all(
        d_cross_ctx, "seq", split_axis=2, concat_axis=1, tiled=True
    ).reshape(row_count, full_len, head_pairs, HEAD)

    def cross_reverse(packed):
        query_row, pair_row, segments, mem_row, log_total, d_row = packed
        d_query, d_key, d_value = attend_backward(
            query_row,
            pair_row[:, 0],
            pair_row[:, 1],
            cross_mask(segments, mem_row),
            log_total,
            d_row,
        )
        return (d_query, jnp.stack((d_key, d_value), axis=1))

    d_query_heads, d_pair_heads = lax.map(
        cross_reverse, (query_heads, pair_heads, seg_ids, mem_segments, cross_lse, d_cross_heads)
    )
    cross_back = (
        lax.all_to_all(
            d_query_heads.reshape(row_count, full_len, 1, head_part),
            "seq",
            split_axis=1,
            concat_axis=3,
            tiled=True,
        ),
        lax.all_to_all(
            d_pair_heads.reshape(row_count, mem_full, 2, head_part),
            "seq",
            split_axis=1,
            concat_axis=3,
            tiled=True,
        ),
    )
    d_query_tok = cross_back[0].reshape(-1, model_width)
    d_pair_tok = cross_back[1].reshape(-1, 2 * model_width)
    d_cross_query = outer_sum(first_low, d_query_tok)
    d_cross_pair = outer_sum(memory_low, d_pair_tok)
    memory_grad = project_back(d_pair_tok, cross_pair).reshape(row_count, mem_span, model_width)
    d_first = d_two + project_back(d_query_tok, cross_query)
    d_one, gain_one, shift_one = norm_backward(d_first, normed_one, inverse_one, gain_rows[0])
    d_attn = d_one.astype(jnp.bfloat16)
    d_self_proj = outer_sum(ctx_low, d_attn)
    d_self_ctx = (
        project_back(d_attn, self_proj)
        .astype(jnp.bfloat16)
        .reshape(row_count, tok_span, model_width)
    )
    d_self_heads = lax.all_to_all(
        d_self_ctx, "seq", split_axis=2, concat_axis=1, tiled=True
    ).reshape(row_count, full_len, head_pairs, HEAD)

    def self_reverse(packed):
        qkv_row, segments, log_total, d_row = packed
        d_query, d_key, d_value = attend_backward(
            qkv_row[:, 0], qkv_row[:, 1], qkv_row[:, 2], self_mask(segments), log_total, d_row
        )
        return jnp.stack((d_query, d_key, d_value), axis=1)

    d_qkv_heads = lax.map(self_reverse, (qkv_split, seg_ids, self_lse, d_self_heads))
    self_back = lax.all_to_all(
        d_qkv_heads.reshape(row_count, full_len, 3, head_part),
        "seq",
        split_axis=1,
        concat_axis=3,
        tiled=True,
    )
    d_qkv_tok = self_back.reshape(-1, 3 * model_width)
    d_self_qkv = outer_sum(input_low, d_qkv_tok)
    input_grad = (d_three + d_one + project_back(d_qkv_tok, self_qkv)).reshape(
        row_count, tok_span, model_width
    )
    gain_grads = jnp.stack((gain_one, gain_two, gain_three), axis=0)
    shift_grads = jnp.stack((shift_one, shift_two, shift_three, ffn_shift), axis=0)
    summed = (
        lax.psum_scatter(d_self_qkv, ("dp", "seq"), scatter_dimension=0, tiled=True),
        lax.psum_scatter(d_self_proj, ("dp", "seq"), scatter_dimension=0, tiled=True),
        lax.psum_scatter(d_cross_query, ("dp", "seq"), scatter_dimension=0, tiled=True),
        lax.psum_scatter(d_cross_pair, ("dp", "seq"), scatter_dimension=0, tiled=True),
        lax.psum_scatter(d_cross_proj, ("dp", "seq"), scatter_dimension=0, tiled=True),
        lax.psum_scatter(d_up, ("dp", "seq"), scatter_dimension=0, tiled=True),
        lax.psum_scatter(d_bias, ("dp", "seq"), scatter_dimension=0, tiled=True),
        lax.psum_scatter(d_down, ("dp", "seq"), scatter_dimension=0, tiled=True),
        lax.psum_scatter(gain_grads, ("dp", "seq"), scatter_dimension=1, tiled=True),
        lax.psum_scatter(shift_grads, ("dp", "seq"), scatter_dimension=1, tiled=True),
    )
    return (
        output,
        input_grad,
        memory_grad,
        summed[0],
        summed[1],
        summed[2],
        summed[3],
        summed[4],
        summed[5],
        summed[6],
        summed[7],
        summed[8],
        summed[9],
    )


def solution(mesh):
    placed = (
        P("dp", "seq", None),
        P("dp", "seq", None),
        P("dp", None),
        P("dp", None),
        P("dp", "seq", None),
        P(("dp", "seq"), None),
        P(("dp", "seq"), None),
        P(("dp", "seq"), None),
        P(("dp", "seq"), None),
        P(("dp", "seq"), None),
        P(("dp", "seq"), None),
        P(("dp", "seq")),
        P(("dp", "seq"), None),
        P(None, ("dp", "seq")),
        P(None, ("dp", "seq")),
    )
    return jax.shard_map(
        on_device,
        mesh=mesh,
        in_specs=placed,
        out_specs=(
            P("dp", "seq", None),
            P("dp", "seq", None),
            P("dp", "seq", None),
            P(("dp", "seq"), None),
            P(("dp", "seq"), None),
            P(("dp", "seq"), None),
            P(("dp", "seq"), None),
            P(("dp", "seq"), None),
            P(("dp", "seq"), None),
            P(("dp", "seq")),
            P(("dp", "seq"), None),
            P(None, ("dp", "seq")),
            P(None, ("dp", "seq")),
        ),
        check_vma=False,
    )
```

profile of v0, /device:TPU:0, one launch (start us, length us, event | category | flops | bytes accessed | tf_op | source)
XLA Modules:
  0.0 1987.5 jit_solution(9784422642280429609)
XLA Ops:
  7.9 60.6 %all-gather.7.cloned.1.call-done = bf16[512,1536]{1,0:T(8,128)(2,1)} async-done(((bf16[16,1536]{1,0:T(8,128)(2,1)}), bf16[512,1536]{1,0:T(8,128)(2,1)}) %all-gather.7.cloned.1.call-update) | async-done | bytes 1572880 | tf_op jit(solution)/shard_map/all_gather | solution.py:100
  97.6 68.1 %all-gather = bf16[32,16,3]{1,2,0:T(4,128)(2,1)S(1)} all-gather(bf16[1,16,3]{1,2,0:T(4,128)(2,1)S(1)} %bitcast.446), channel_id=1, replica_groups=mesh['dp'=8,'seq'=4] {'dp','seq'}, dimensions={0}, use_global_device_ids=true | all-gather | bytes 3168 | tf_op jit(solution)/shard_map/all_gather | solution.py:108
  165.8 36.8 %all-gather.1 = bf16[32,16,4]{1,2,0:T(4,128)(2,1)S(1)} all-gather(bf16[1,16,4]{1,2,0:T(4,128)(2,1)S(1)} %bitcast.447), channel_id=1, replica_groups=mesh['dp'=8,'seq'=4] {'dp','seq'}, dimensions={0}, use_global_device_ids=true | all-gather | bytes 4224 | tf_op jit(solution)/shard_map/all_gather | solution.py:109
  215.8 34.4 %while.46 = (s32[]{:T(128)}, bf16[4,1024,2,64]{1,3,2,0:T(8,128)(2,1)S(1)}, f32[4,2,1024,1]{2,1,3,0:T(2,128)S(1)}, bf16[4,1024,3,2,64]{1,4,3,2,0:T(8,128)(2,1)}, s32[4,1024]{1,0:T(4,128)S(1)}, /*index=5*/s32[]{:T(128)}) while((s32[]{:T(128)}, bf16[4,1024,2,64]{1,3,2,0:T(8,128)(2,1)S(1)}, f32[4,2,1024,1]{2,1,3,0:T(2,128)S(1)}, ...), condition=%wide.region_3.4_spmd, body=%wide.region_0.3_spmd.sunk | while | flops 565311488 | bytes 32059484 | solution.py:140
  256.0 48.3 %all_gather.31 = bf16[512,512]{1,0:T(8,128)(2,1)} all-gather(bf16[16,512]{1,0:T(8,128)(2,1)S(1)} %copy-done.39), channel_id=1, replica_groups=mesh['dp'=8,'seq'=4] {'dp','seq'}, dimensions={0}, use_global_device_ids=true | all-gather | bytes 540672 | tf_op jit(solution)/shard_map/all_gather | solution.py:101
  320.0 56.9 %all_gather.35 = bf16[512,512]{1,0:T(8,128)(2,1)S(1)} all-gather(bf16[16,512]{1,0:T(8,128)(2,1)S(1)} %copy-done.40), channel_id=1, replica_groups=mesh['dp'=8,'seq'=4] {'dp','seq'}, dimensions={0}, use_global_device_ids=true | all-gather | bytes 540672 | tf_op jit(solution)/shard_map/all_gather | solution.py:102
  410.7 36.3 %while.47 = (s32[]{:T(128)}, bf16[4,1024,2,64]{1,3,2,0:T(8,128)(2,1)}, f32[4,2,1024,1]{2,1,3,0:T(2,128)S(1)}, bf16[4,1024,2,2,64]{1,4,3,2,0:T(8,128)(2,1)S(1)}, ...) while((s32[]{:T(128)}, ...), condition=%wide.region_11.12_spmd, body=%wide.region_8.11_spmd.sunk | while | flops 563214336 | bytes 31547504 | solution.py:182
  454.7 45.5 %all-reduce = bf16[2048]{0:T(1024)(128)(2,1)S(1)} all-reduce(bf16[2048]{0:T(1024)(128)(2,1)S(1)} %dynamic-update-slice), channel_id=1, replica_groups=mesh['dp'=8,'seq'=4] {'dp','seq'}, use_global_device_ids=true, to_apply=%add | all-reduce | flops 2048 | bytes 8192
  502.6 45.7 %all_gather.36 = bf16[512,512]{1,0:T(8,128)(2,1)} all-gather(bf16[16,512]{1,0:T(8,128)(2,1)S(1)} %copy-done.41), channel_id=1, replica_groups=mesh['dp'=8,'seq'=4] {'dp','seq'}, dimensions={0}, use_global_device_ids=true | all-gather | bytes 540672 | tf_op jit(solution)/shard_map/all_gather | solution.py:104
  590.9 14.4 all-to-all-done.5
  609.1 164.4 %while.48 = (s32[]{:T(128)}, bf16[4,1024,2,64]{1,3,2,0:T(8,128)(2,1)}, bf16[4,1024,2,2,64]{1,4,3,2,0:T(8,128)(2,1)}, bf16[4,1024,2,2,64]{1,4,3,2,0:T(8,128)(2,1)...) while((s32[]{:T(128)}, ...), condition=%wide.region_22.23_spmd, body=%wide.region_20.22_spmd.sunk | while | flops 1399199744 | bytes 141115584 | solution.py:238
  621.0 13.9 fusion.297
  634.9 14.5 fusion.295
  676.1 14.5 fusion.295
  703.2 13.9 fusion.297
  717.1 14.5 fusion.295
  758.2 14.5 fusion.295
  776.1 18.2 all_to_all.150
  817.6 28.6 %all_to_all.151 = bf16[4,1024,2,128]{3,2,0,1:T(2,128)(2,1)S(1)} all-to-all(bf16[4,1024,2,128]{3,2,0,1:T(2,128)(2,1)S(1)} %copy.281), channel_id=1, replica_groups=mesh['dp'=8,'seq'=4] {'seq'}, dimensions={1} | all-to-all | bytes 4194304 | tf_op jit(solution)/shard_map/all_to_all | solution.py:249
  898.1 167.6 %while.49 = (s32[]{:T(128)}, bf16[4,1024,3,2,64]{1,4,3,2,0:T(8,128)(2,1)}, bf16[4,1024,3,2,64]{1,4,3,2,0:T(8,128)(2,1)}, s32[4,1024]{1,0:T(4,128)S(1)}, f32[4,2,...) while((s32[]{:T(128)}, bf16[4,1024,3,2,64]{1,4,3,2,0:T(8,128)(2,1)}, ...), condition=%wide.region_27.28_spmd, body=%wide.region_25.27_spmd.sunk | while | flops 1402607616 | bytes 142151856 | solution.py:282
  923.5 14.6 fusion.308
  965.4 14.6 fusion.308
  1007.3 14.6 fusion.308
  1049.2 14.6 fusion.308
  1071.8 43.9 %all_to_all.152 = bf16[4,1024,3,128]{3,0,2,1:T(4,128)(2,1)S(1)} all-to-all(bf16[4,1024,3,128]{3,0,2,1:T(4,128)(2,1)} %copy.278), channel_id=1, replica_groups=mesh['dp'=8,'seq'=4] {'seq'}, dimensions={1} | all-to-all | bytes 6291456 | tf_op jit(solution)/shard_map/all_to_all | solution.py:283
  1136.2 36.9 %all-reduce.1 = f32[2048]{0:T(1024)S(1)} all-reduce(f32[2048]{0:T(1024)S(1)} %copy-done.47), channel_id=8, replica_groups=mesh['dp'=8,'seq'=4] {'dp','seq'}, use_global_device_ids=true, to_apply=%region_35.36.clone | all-reduce | flops 2048 | bytes 16384
  1195.6 133.7 %reduce-scatter.20.cloned.1.call-done = f32[16,512]{1,0:T(8,128)} async-done(((f32[512,512]{1,0:T(8,128)}), f32[16,512]{1,0:T(8,128)}) %reduce-scatter.20.cloned.1.call-update) | async-done | bytes 32784 | tf_op jit(solution)/shard_map/reduce_scatter | solution.py:300
  1329.2 133.6 %reduce-scatter.18.cloned.1.call-done = f32[16,512]{1,0:T(8,128)} async-done(((f32[512,512]{1,0:T(8,128)}), f32[16,512]{1,0:T(8,128)}) %reduce-scatter.18.cloned.1.call-update) | async-done | bytes 32784 | tf_op jit(solution)/shard_map/reduce_scatter | solution.py:299
  1462.8 135.4 %reduce-scatter.30.cloned.1.call-done = f32[16,1024]{1,0:T(8,128)} async-done(((f32[512,1024]{1,0:T(8,128)}), f32[16,1024]{1,0:T(8,128)}) %reduce-scatter.30.cloned.1.call-update) | async-done | bytes 65552
  1598.2 139.7 %reduce-scatter.26.cloned.1.call-done = f32[64,512]{1,0:T(8,128)} async-done(((f32[2048,512]{1,0:T(8,128)}), f32[64,512]{1,0:T(8,128)}) %reduce-scatter.26.cloned.1.call-update) | async-done | bytes 131088 | tf_op jit(solution)/shard_map/reduce_scatter | solution.py:305
  1737.9 139.3 %reduce-scatter.24.cloned.1.call-done = f32[16,2048]{1,0:T(8,128)} async-done(((f32[512,2048]{1,0:T(8,128)}), f32[16,2048]{1,0:T(8,128)}) %reduce-scatter.24.cloned.1.call-update) | async-done | bytes 131088 | tf_op jit(solution)/shard_map/reduce_scatter | solution.py:303
  1877.2 103.6 %reduce-scatter.28.cloned.1.call-done = f32[16,1536]{1,0:T(8,128)} async-done(((f32[512,1536]{1,0:T(8,128)}), f32[16,1536]{1,0:T(8,128)}) %reduce-scatter.28.cloned.1.call-update) | async-done | bytes 98320
  (418 shorter events, 538.4 us)
Async XLA Ops:
  7.2 297.1 %copy-start = (bf16[4,256,512]{2,1,0:T(8,128)(2,1)S(1)}, bf16[4,256,512]{2,1,0:T(8,128)(2,1)}, u32[]{:S(2)}) copy-start(bf16[4,256,512]{2,1,0:T(8,128)(2,1)} %param.24) | copy-start | bytes 3145732
  7.2 61.4 %all-gather.7.cloned.1.call-start = ((), (), s32[]{:S(2)}) async-start(), calls=%async_computation.19 | async-start | bytes 1622016 | tf_op jit(solution)/shard_map/all_gather | solution.py:100
  91.3 74.4 %copy-start.52 = (bf16[4,16]{1,0:T(4,128)(2,1)S(1)}, bf16[4,16]{1,0:T(4,128)(2,1)}, u32[]{:S(2)}) copy-start(bf16[4,16]{1,0:T(4,128)(2,1)} %param.37) | copy-start | bytes 388
  91.3 111.7 %all-to-all-start = ((bf16[4,256,3,512]{1,0,2,3:T(4,128)(2,1)}), bf16[4,256,3,512]{1,0,2,3:T(4,128)(2,1)}, u32[]{:S(2)}, u32[]{:S(2)}) async-start(bf16[4,256,3,512]{1,0,2,3:T(4,128)(2,1)} %copy.253), calls=%async_computation | async-start | bytes 6291456 | tf_op jit(solution)/shard_map/all_to_all | solution.py:133
  96.1 208.2 %all-gather.9.cloned.1.call-start = ((), (), s32[]{:S(2)}) async-start(), calls=%async_computation.20 | async-start | bytes 1081344 | tf_op jit(solution)/shard_map/all_gather | solution.py:103
  96.9 455.3 %all-gather.11.cloned.1.call-start = ((), (), s32[]{:S(2)}) async-start(), calls=%async_computation.21 | async-start | bytes 2162688 | tf_op jit(solution)/shard_map/all_gather | solution.py:105
  250.2 54.1 %copy-start.34 = (f32[4,2,1024,1]{2,1,3,0:T(2,128)}, f32[4,2,1024,1]{2,1,3,0:T(2,128)S(1)}, u32[]{:S(2)}) copy-start(f32[4,2,1024,1]{2,1,3,0:T(2,128)S(1)} %get-tuple-element.624) | copy-start | bytes 98308
  251.7 64.5 %all-to-all-start.1 = ((bf16[4,1024,128]{2,0,1:T(4,128)(2,1)}), bf16[4,1024,128]{2,0,1:T(4,128)(2,1)}, u32[]{:S(2)}, u32[]{:S(2)}) async-start(bf16[4,1024,128]{2,0,1:T(4,128)(2,1)} %copy.256), calls=%async_computation.1 | async-start | bytes 2097152 | tf_op jit(solution)/shard_map/all_to_all | solution.py:141
  255.9 294.7 %copy-start.49 = (f32[1,512]{1,0:T(1,128)}, f32[1,512]{1,0:T(1,128)S(1)}, u32[]{:S(2)}) copy-start(f32[1,512]{1,0:T(1,128)S(1)} %get-tuple-element.353) | copy-start | bytes 6148
  255.9 303.7 %copy-start.37 = (f32[1,512]{1,0:T(1,128)}, f32[1,512]{1,0:T(1,128)S(1)}, u32[]{:S(2)}) copy-start(f32[1,512]{1,0:T(1,128)S(1)} %get-tuple-element.352) | copy-start | bytes 6148
  316.2 68.6 %all-to-all-start.2 = ((bf16[4,256,2,512]{1,0,2,3:T(4,128)(2,1)}), bf16[4,256,2,512]{1,0,2,3:T(4,128)(2,1)S(1)}, u32[]{:S(2)}, u32[]{:S(2)}) async-start(bf16[4,256,2,512]{1,0,2,3:T(4,128)(2,1)} %copy.263), calls=%async_computation.2 | async-start | bytes 4194304 | tf_op jit(solution)/shard_map/all_to_all | solution.py:166
  319.9 59.4 %copy-start.23 = (bf16[512,512]{1,0:T(8,128)(2,1)S(1)}, bf16[512,512]{1,0:T(8,128)(2,1)}, u32[]{:S(2)}) copy-start(bf16[512,512]{1,0:T(8,128)(2,1)} %all_gather.31) | copy-start | bytes 1572868
  319.9 59.4 %copy-start.29 = (bf16[4,256,512]{2,1,0:T(8,128)(2,1)S(1)}, bf16[4,256,512]{2,1,0:T(8,128)(2,1)}, u32[]{:S(2)}) copy-start(bf16[4,256,512]{2,1,0:T(8,128)(2,1)} %param.23) | copy-start | bytes 3145732
  319.9 230.7 %copy-start.44 = (f32[1,512]{1,0:T(1,128)}, f32[1,512]{1,0:T(1,128)S(1)}, u32[]{:S(2)}) copy-start(f32[1,512]{1,0:T(1,128)S(1)} %get-tuple-element.349) | copy-start | bytes 6148
  380.1 170.5 %copy-start.35 = (f32[1024]{0:T(1024)}, f32[1024]{0:T(1024)S(1)}, u32[]{:S(2)}) copy-start(f32[1024]{0:T(1024)S(1)} %broadcast_multiply_fusion.7) | copy-start | bytes 12292
  380.6 170.1 %copy-start.42 = (f32[1024]{0:T(1024)}, f32[1024]{0:T(1024)S(1)}, u32[]{:S(2)}) copy-start(f32[1024]{0:T(1024)S(1)} %add_rsqrt_fusion.2) | copy-start | bytes 12292
  384.8 19.3 all-to-all-start.3
  389.1 170.6 %all-gather.13.cloned.1.call-start = ((), (), s32[]{:S(2)}) async-start(), calls=%async_computation.22 | async-start | bytes 2162688 | tf_op jit(solution)/shard_map/all_gather | solution.py:107
  447.1 102.7 %copy-start.5 = (bf16[4,1024,2,2,64]{1,4,3,2,0:T(8,128)(2,1)}, bf16[4,1024,2,2,64]{1,4,3,2,0:T(8,128)(2,1)S(1)}, u32[]{:S(2)}) copy-start(bf16[4,1024,2,2,64]{1,4,3,2,0:T(8,128)(2,1)S(1)} %get-tuple-element.655) | copy-start | bytes 6291460
  447.1 55.5 %copy-start.41 = (bf16[16,512]{1,0:T(8,128)(2,1)S(1)}, bf16[16,512]{1,0:T(8,128)(2,1)}, u32[]{:S(2)}) copy-start(bf16[16,512]{1,0:T(8,128)(2,1)} %param.32) | copy-start | bytes 49156
  450.1 98.1 %all-to-all-start.4 = ((bf16[4,1024,128]{2,0,1:T(4,128)(2,1)}), bf16[4,1024,128]{2,0,1:T(4,128)(2,1)}, u32[]{:S(2)}, u32[]{:S(2)}) async-start(bf16[4,1024,128]{2,0,1:T(4,128)(2,1)} %copy.268), calls=%async_computation.4 | async-start | bytes 2097152 | tf_op jit(solution)/shard_map/all_to_all | solution.py:183
  587.3 18.0 all-to-all-start.5
  590.8 582.8 %reduce-scatter.32.cloned.1.call-start = ((), (), s32[]{:S(2)}) async-start(), calls=%async_computation.30 | async-start | bytes 270336
  799.3 375.8 %reduce-scatter.34.cloned.1.call-start = ((), (), s32[]{:S(2)}) async-start(), calls=%async_computation.31 | async-start | bytes 270336
  800.2 395.3 %reduce-scatter.22.cloned.1.call-start = ((), (), s32[]{:S(2)}) async-start(), calls=%async_computation.25 | async-start | bytes 1081344 | tf_op jit(solution)/shard_map/reduce_scatter | solution.py:302
  803.2 526.0 %reduce-scatter.20.cloned.1.call-start = ((), (), s32[]{:S(2)}) async-start(), calls=%async_computation.24 | async-start | bytes 1081344 | tf_op jit(solution)/shard_map/reduce_scatter | solution.py:300
  807.4 655.4 %reduce-scatter.18.cloned.1.call-start = ((), (), s32[]{:S(2)}) async-start(), calls=%async_computation.23 | async-start | bytes 1081344 | tf_op jit(solution)/shard_map/reduce_scatter | solution.py:299
  812.8 785.4 %reduce-scatter.30.cloned.1.call-start = ((), (), s32[]{:S(2)}) async-start(), calls=%async_computation.29 | async-start | bytes 2162688
  858.3 879.6 %reduce-scatter.26.cloned.1.call-start = ((), (), s32[]{:S(2)}) async-start(), calls=%async_computation.27 | async-start | bytes 4325376 | tf_op jit(solution)/shard_map/reduce_scatter | solution.py:305
  875.1 19.0 all-to-all-start.7
  879.3 997.8 %reduce-scatter.24.cloned.1.call-start = ((), (), s32[]{:S(2)}) async-start(), calls=%async_computation.26 | async-start | bytes 4325376 | tf_op jit(solution)/shard_map/reduce_scatter | solution.py:303
  886.2 1094.6 %reduce-scatter.28.cloned.1.call-start = ((), (), s32[]{:S(2)}) async-start(), calls=%async_computation.28 | async-start | bytes 3244032
  (58 other events, 384.7 us)
Sparse Core Ops, SparseCore 0:
  10.9 57.6 all-gather.6
  99.8 54.5 all-gather.8
  157.3 55.4 all-gather.10
  392.4 54.1 all-gather.12
  799.4 129.6 reduce-scatter.31
  931.2 129.4 reduce-scatter.33
  1063.5 132.0 reduce-scatter.21
  1198.5 130.7 reduce-scatter.19
  1332.0 130.7 reduce-scatter.17
  1465.6 132.5 reduce-scatter.29
  1601.0 136.8 reduce-scatter.25
  1740.6 136.5 reduce-scatter.23
  1883.2 97.5 reduce-scatter.27
where the time goes:
time: 1990 us
  waiting for transfers between devices  886 us (45%)
  matrix products  433 us (22%)
  blocking collectives  429 us (22%)
  local copies, waits for them, and re-layouts  147 us (7%)
  other arithmetic  47.3 us (2%)
  starting transfers between devices  29.8 us (1%)
    unnamed x17, waiting for transfers between devices  242 us
    reduce_scatter x1, waiting for transfers between devices, on_device(): lax.psum_scatter(d_down, ('dp', 'seq'), scatter_dimension=0, tiled=True)  140 us
    reduce_scatter x1, waiting for transfers between devices, on_device(): lax.psum_scatter(d_up, ('dp', 'seq'), scatter_dimension=0, tiled=True)  139 us
    reduce_scatter x1, waiting for transfers between devices, on_device(): lax.psum_scatter(d_cross_query, ('dp', 'seq'), scatter_dimension=0, tiled...  134 us
    reduce_scatter x1, waiting for transfers between devices, on_device(): lax.psum_scatter(d_self_proj, ('dp', 'seq'), scatter_dimension=0, tiled=T...  134 us
    dot_general x8, matrix products, attend_backward(): jnp.einsum('pqk,qpe->kpe', d_scores, query_rows, preferred_element_type=j...  114 us
    dot_general x8, matrix products, attend_backward(): jnp.einsum('pqk,kpe->qpe', d_scores, key_rows, preferred_element_type=jnp...  113 us
    unnamed x2, blocking collectives  82.4 us
  transfers between devices with their start and end apart: 20, of which 11 were waited for; matrix products, arithmetic and copies ran while one was open for 20% of the time, Pallas kernels for 0%

commit v1 on v0

v1 whole, which is shorter than its diff:
```python
import functools

import jax
import jax.numpy as jnp
from jax import lax
from jax.experimental import pallas as pl
from jax.experimental.pallas import tpu as pltpu
from jax.sharding import PartitionSpec as P

HEAD = 64
PAIR = 2 * HEAD
TILE = 256
FAST = 32
AXES = ("dp", "seq")
LOG2E = 1.4426950408889634
AWAY = -1e30
GELU_A = 0.7978845608028654
GELU_B = 0.044715
BF = jnp.bfloat16
F4 = jnp.float32
VMEM_BYTES = 58 << 20


def mm(a, b):
    return lax.dot_general(a, b, (((1,), (0,)), ((), ())), preferred_element_type=F4)


def mt(a, b):
    return lax.dot_general(a, b, (((1,), (1,)), ((), ())), preferred_element_type=F4)


def tm(a, b):
    return lax.dot_general(a, b, (((0,), (0,)), ((), ())), preferred_element_type=F4)


def any_spec():
    return pl.BlockSpec(memory_space=pl.ANY)


def smem_spec():
    return pl.BlockSpec(memory_space=pltpu.SMEM)


def struct(shape, dtype):
    return jax.ShapeDtypeStruct(shape, dtype)


def params(**more):
    return pltpu.CompilerParams(vmem_limit_bytes=VMEM_BYTES, **more)


def cost(flops, bytes_accessed):
    return pl.CostEstimate(flops=int(flops), bytes_accessed=int(bytes_accessed), transcendentals=0)


def rel(p):
    return ((p % 4) << 3) | (((p >> 2) & 1) << 1) | (((p >> 3) & 1) << 2) | (p >> 4)


def wait_all(buffer, sem):
    pltpu.make_async_copy(buffer, buffer, sem).wait()


def start_rows(dst, own, got, seat, sem):
    span = own.shape[1]
    for r in range(len(got) + 1):
        src = own.at[seat] if r == 0 else got[r - 1]
        place = pl.multiple_of((seat ^ r) * span, span)
        pltpu.make_async_copy(src, dst.at[pl.ds(place, span)], sem).start()


def start_weight(dst, parts, first, me, sem):
    rows, columns = dst.shape
    if len(parts) == 1:
        pltpu.make_async_copy(parts[0].at[:, pl.ds(first, columns)], dst, sem).start()
        return
    span = rows // FAST
    for p in range(FAST):
        place = pl.multiple_of((me ^ rel(p)) * span, span)
        src = parts[p // 16].at[pl.ds((p % 16) * span, span), pl.ds(first, columns)]
        pltpu.make_async_copy(src, dst.at[pl.ds(place, span)], sem).start()


def start_grad(src, parts, me, sem):
    if len(parts) == 1:
        pltpu.make_async_copy(src, parts[0], sem).start()
        return
    span = src.shape[0] // FAST
    for p in range(FAST):
        place = pl.multiple_of((me ^ rel(p)) * span, span)
        dst = parts[p // 16].at[pl.ds((p % 16) * span, span)]
        pltpu.make_async_copy(src.at[pl.ds(place, span)], dst, sem).start()


def start_blocks(src, outs, seat, sem):
    span = outs[0].shape[0]
    for r, out in enumerate(outs):
        place = pl.multiple_of((seat ^ r) * span, span)
        pltpu.make_async_copy(src.at[pl.ds(place, span)], out, sem).start()


def grad_shapes(rows, columns, fast):
    if fast:
        return [struct((rows // 2, columns), BF)] * 2
    return [struct((rows, columns), BF)]


def norm(values):
    centered = values - jnp.mean(values, axis=-1, keepdims=True)
    inverse = lax.rsqrt(jnp.mean(centered * centered, axis=-1, keepdims=True) + 1e-05)
    return centered * inverse, inverse


def norm_back(upstream, normed, inverse, gain_row):
    gain_part = jnp.sum(upstream * normed, axis=0, keepdims=True)
    shift_part = jnp.sum(upstream, axis=0, keepdims=True)
    scaled = upstream * gain_row
    centered = scaled - jnp.mean(scaled, axis=-1, keepdims=True)
    value = inverse * (centered - normed * jnp.mean(scaled * normed, axis=-1, keepdims=True))
    return value, gain_part, shift_part


def lane_masks(dtype):
    lane = lax.broadcasted_iota(jnp.int32, (1, PAIR), 1)
    own = [(lane // HEAD == h).astype(dtype) for h in range(2)]

    def spot(h, k):
        return ((lane // HEAD == 1 - h) & (lane % HEAD == k)).astype(dtype)

    return own, spot


def attend_pair(causal, query, key, value, augq, augk, tri, ctx_out, qa_out, ka_out):
    total = key.shape[0]
    own, spot = lane_masks(F4)
    own_low = [mask.astype(BF) for mask in own]
    eighth = [(mask * HEAD ** (-0.5)).astype(BF) for mask in own]
    wide = jnp.concatenate([value, jnp.ones((total, PAIR), BF)], axis=1)
    keys = []
    for h in range(2):
        keys.append(key * own_low[h] + augk[h])
        ka_out[h] = keys[h]
    units = [(i, h) for i in range(query.shape[0] // TILE) for h in range(2)]
    scores, probs, halves = {}, {}, {}

    def score(i, h):
        rows = slice(i * TILE, (i + 1) * TILE)
        width = (i + 1) * TILE if causal else total
        head = query[rows] * eighth[h] + augq[h, rows]
        s = mt(head, keys[h][:width])
        if causal:
            tail = s[:, width - TILE :] + tri[...]
            s = jnp.concatenate([s[:, : width - TILE], tail], axis=1) if i else tail
        return s, head

    def finish(i, h, low, top, head):
        rows = slice(i * TILE, (i + 1) * TILE)
        both = mm(low, wide[: low.shape[1]])
        sums = both[:, PAIR:]
        halves[h] = both[:, :PAIR] / sums
        rest = -(top + jnp.log(sums))
        high = rest.astype(BF).astype(F4)
        rest = rest - high
        middle = rest.astype(BF).astype(F4)
        extra = high * spot(h, 8) + middle * spot(h, 9) + (rest - middle) * spot(h, 10)
        qa_out[h, rows] = head + extra.astype(BF)
        if h == 1:
            ctx_out[rows] = (halves[0] * own[0] + halves[1] * own[1]).astype(BF)

    count = len(units)
    for t in range(count + 2):
        if t < count:
            scores[t] = score(*units[t])
        if 0 <= t - 2 < count:
            finish(*units[t - 2], *probs.pop(t - 2))
        if 0 <= t - 1 < count:
            s, head = scores.pop(t - 1)
            top = jnp.max(s, axis=1, keepdims=True)
            low = jnp.exp2(s * LOG2E - top * LOG2E).astype(BF)
            probs[t - 1] = (low, top, head)


def self_forward_kernel(seats, nparts, *refs):
    place, own = refs[0], refs[1]
    got = refs[2 : 1 + seats]
    rest = refs[1 + seats :]
    parts = rest[:nparts]
    augq, augk, tri, ctx, qa, ka, vo, x_v, w_v, qkv, sems = rest[nparts:]
    pair = pl.program_id(0)
    width = x_v.shape[1]

    @pl.when(pair == 0)
    def _():
        seat, me = place[0], place[1]
        start_rows(x_v, own, got, seat, sems.at[0])
        start_weight(w_v, parts, 0, me, sems.at[1])
        wait_all(x_v, sems.at[0])
        wait_all(w_v, sems.at[1])
        for c in range(0, 3 * width, 512):
            qkv[:, c : c + 512] = mm(x_v[...], w_v[:, c : c + 512]).astype(BF)

    def columns(part):
        return qkv[:, pl.ds(pl.multiple_of(part * width + pair * PAIR, PAIR), PAIR)]

    value = columns(2)
    vo[...] = value
    attend_pair(True, columns(0), columns(1), value, augq, augk, tri, ctx, qa, ka)


def self_forward(place, own, got, parts, augq, augk, tri):
    seats, span, width = own.shape
    full = seats * span
    heads = width // HEAD
    both = pl.BlockSpec((2, full, PAIR), lambda p: (p, 0, 0))
    cols = pl.BlockSpec((full, PAIR), lambda p: (0, p))
    return pl.pallas_call(
        functools.partial(self_forward_kernel, seats, len(parts)),
        name="self_forward",
        grid=(heads // 2,),
        in_specs=[smem_spec()]
        + [any_spec()] * (seats + len(parts))
        + [
            pl.BlockSpec((2, full, PAIR), lambda p: (0, 0, 0)),
            pl.BlockSpec((2, full, PAIR), lambda p: (0, 0, 0)),
            pl.BlockSpec((TILE, TILE), lambda p: (0, 0)),
        ],
        out_specs=[cols, both, both, cols],
        out_shape=[
            struct((full, width), BF),
            struct((heads, full, PAIR), BF),
            struct((heads, full, PAIR), BF),
            struct((full, width), BF),
        ],
        scratch_shapes=[
            pltpu.VMEM((full, width), BF),
            pltpu.VMEM((width, 3 * width), BF),
            pltpu.VMEM((full, 3 * width), BF),
            pltpu.SemaphoreType.DMA((2,)),
        ],
        compiler_params=params(),
        cost_estimate=cost(11e9, 8e6),
    )(place, own, *got, *parts, augq, augk, tri)


def cross_forward_kernel(seats, nparts, *refs):
    place, x_own = refs[0], refs[1]
    x_got = refs[2 : 1 + seats]
    mem_own = refs[1 + seats]
    mem_got = refs[2 + seats : 1 + 2 * seats]
    rest = refs[1 + 2 * seats :]
    parts = rest[:nparts]
    (ctx, vec, augq, augk, cctx, qa, ka, vo, xhat, inv, x_v, m_v, w_v, q_v, kv, sems) = rest[nparts:]
    pair = pl.program_id(0)
    full, width = x_v.shape

    @pl.when(pair == 0)
    def _():
        seat, me = place[0], place[1]
        start_weight(w_v, parts, 0, me, sems.at[0])
        start_rows(x_v, x_own, x_got, seat, sems.at[1])
        start_rows(m_v, mem_own, mem_got, seat, sems.at[2])
        wait_all(w_v, sems.at[0])
        wait_all(x_v, sems.at[1])
        for i in range(0, full, TILE):
            rows = slice(i, i + TILE)
            attn = mm(ctx[rows], w_v[:, :width])
            normed, inverse = norm(x_v[rows].astype(F4) + attn)
            xhat[rows] = normed
            inv[rows] = jnp.broadcast_to(inverse, (TILE, PAIR))
            first = (normed * vec[0:1] + vec[3:4]).astype(BF)
            q_v[rows] = mm(first, w_v[:, width : 2 * width]).astype(BF)
        wait_all(m_v, sems.at[2])
        for c in range(0, 2 * width, 512):
            kv[:, c : c + 512] = mm(m_v[...], w_v[:, 2 * width + c : 2 * width + c + 512]).astype(BF)

    lanes = pl.ds(pl.multiple_of(pair * PAIR, PAIR), PAIR)
    late = pl.ds(pl.multiple_of(width + pair * PAIR, PAIR), PAIR)
    value = kv[:, late]
    vo[...] = value
    attend_pair(False, q_v[:, lanes], kv[:, lanes], value, augq, augk, None, cctx, qa, ka)


def cross_forward(place, x_own, x_got, mem_own, mem_got, parts, ctx, vec, augq, augk):
    seats, span, width = x_own.shape
    full = seats * span
    heads = width // HEAD
    both = pl.BlockSpec((2, full, PAIR), lambda p: (p, 0, 0))
    cols = pl.BlockSpec((full, PAIR), lambda p: (0, p))
    return pl.pallas_call(
        functools.partial(cross_forward_kernel, seats, len(parts)),
        name="cross_forward",
        grid=(heads // 2,),
        in_specs=[smem_spec()]
        + [any_spec()] * (2 * seats + len(parts))
        + [
            pl.BlockSpec((full, width), lambda p: (0, 0)),
            pl.BlockSpec(vec.shape, lambda p: (0, 0)),
            pl.BlockSpec((2, full, PAIR), lambda p: (0, 0, 0)),
            pl.BlockSpec((2, full, PAIR), lambda p: (0, 0, 0)),
        ],
        out_specs=[
            cols,
            both,
            both,
            cols,
            pl.BlockSpec((full, width), lambda p: (0, 0)),
            pl.BlockSpec((full, PAIR), lambda p: (0, 0)),
        ],
        out_shape=[
            struct((full, width), BF),
            struct((heads, full, PAIR), BF),
            struct((heads, full, PAIR), BF),
            struct((full, width), BF),
            struct((full, width), F4),
            struct((full, PAIR), F4),
        ],
        scratch_shapes=[
            pltpu.VMEM((full, width), BF),
            pltpu.VMEM((full, width), BF),
            pltpu.VMEM((width, 4 * width), BF),
            pltpu.VMEM((full, width), BF),
            pltpu.VMEM((full, 2 * width), BF),
            pltpu.SemaphoreType.DMA((3,)),
        ],
        compiler_params=params(),
        cost_estimate=cost(15e9, 14e6),
    )(place, x_own, *x_got, mem_own, *mem_got, *parts, ctx, vec, augq, augk)


def middle_kernel(seats, nparts, *refs):
    place, x_own = refs[0], refs[1]
    x_got = refs[2 : 1 + seats]
    g_own = refs[1 + seats]
    g_got = refs[2 + seats : 1 + 2 * seats]
    rest = refs[1 + 2 * seats :]
    co_parts, rest = rest[:nparts], rest[nparts:]
    up_parts, rest = rest[:nparts], rest[nparts:]
    down_parts, rest = rest[:nparts], rest[nparts:]
    (cctx, xhat, vec, bias), rest = rest[:4], rest[4:]
    outs, rest = rest[:seats], rest[seats:]
    (d3_o, d2_o, dcctx, vec_o, bias_o), rest = rest[:5], rest[5:]
    upco_g, rest = rest[:nparts], rest[nparts:]
    down_g, rest = rest[:nparts], rest[nparts:]
    (x_v, g_v, co_v, up_v, down_v, out_v, s_v, h_v, dp_v, df_v, dc_v, gu_v, gd_v, sems) = rest
    full, width = x_v.shape
    hidden = up_v.shape[1]
    seat, me = place[0], place[1]
    start_weight(co_v, co_parts, 4 * width, me, sems.at[0])
    start_weight(up_v, up_parts, 0, me, sems.at[1])
    start_weight(down_v, down_parts, 0, me, sems.at[2])
    start_rows(x_v, x_own, x_got, seat, sems.at[3])
    start_rows(g_v, g_own, g_got, seat, sems.at[4])
    vec_o[...] = jnp.zeros(vec_o.shape, F4)
    bias_o[...] = jnp.zeros(bias_o.shape, F4)
    wait_all(co_v, sems.at[0])
    wait_all(up_v, sems.at[1])
    wait_all(down_v, sems.at[2])
    wait_all(x_v, sems.at[3])
    wait_all(g_v, sems.at[4])

    def tile(i, carry):
        rows = pl.ds(pl.multiple_of(i * TILE, TILE), TILE)
        first = xhat[rows] * vec[0:1] + vec[3:4]
        normed_one, inverse_one = norm(first + mm(cctx[rows], co_v[...]))
        second = normed_one * vec[1:2] + vec[4:5]
        low = second.astype(BF)
        s_v[rows] = low
        pre = mm(low, up_v[...]) + bias[...]
        square = pre * pre
        slope = GELU_A * GELU_B * square + GELU_A
        t = jnp.tanh(pre * slope)
        half = 0.5 * t + 0.5
        hid = (pre * half).astype(BF)
        h_v[rows] = hid
        d_gelu = half + (0.5 - 0.5 * t * t) * pre * (3.0 * slope - 2.0 * GELU_A)
        ffn = mm(hid, down_v[...]) + vec[6:7]
        normed_two, inverse_two = norm(second + ffn + x_v[rows].astype(F4))
        out_v[rows] = (normed_two * vec[2:3] + vec[5:6]).astype(BF)
        d_three, gain_two, shift_two = norm_back(g_v[rows].astype(F4), normed_two, inverse_two, vec[2:3])
        d3_o[rows] = d_three
        df = d_three.astype(BF)
        df_v[rows] = df
        d_pre = (mt(df, down_v[...]) * d_gelu).astype(BF)
        dp_v[rows] = d_pre
        bias_o[...] += jnp.sum(d_pre.astype(F4), axis=0, keepdims=True)
        d_second = d_three + mt(d_pre, up_v[...])
        d_two, gain_one, shift_one = norm_back(d_second, normed_one, inverse_one, vec[1:2])
        d2_o[rows] = d_two
        dc = d_two.astype(BF)
        dc_v[rows] = dc
        dcctx[rows] = mt(dc, co_v[...]).astype(BF)
        vec_o[1:2] += gain_one
        vec_o[2:3] += gain_two
        vec_o[4:5] += shift_one
        vec_o[5:6] += shift_two
        vec_o[6:7] += jnp.sum(d_three, axis=0, keepdims=True)
        return carry

    lax.fori_loop(0, full // TILE, tile, 0)
    start_blocks(out_v, outs, seat, sems.at[0])
    for c in range(0, hidden, 512):
        gd_v[c : c + 512] = tm(h_v[:, c : c + 512], df_v[...]).astype(BF)
    start_grad(gd_v, down_g, me, sems.at[1])
    for c in range(0, hidden, 512):
        gu_v[:, c : c + 512] = tm(s_v[...], dp_v[:, c : c + 512]).astype(BF)
    gu_v[:, hidden:] = tm(cctx[...], dc_v[...]).astype(BF)
    start_grad(gu_v, upco_g, me, sems.at[2])
    wait_all(out_v, sems.at[0])
    wait_all(gd_v, sems.at[1])
    wait_all(gu_v, sems.at[2])


def middle(place, x_own, x_got, g_own, g_got, co_parts, up_parts, down_parts, cctx, xhat, vec, bias, fast):
    seats, span, width = x_own.shape
    full = seats * span
    hidden = bias.shape[1]
    whole = pl.BlockSpec(memory_space=pltpu.VMEM)
    nparts = len(co_parts)
    out_shape = (
        [struct((span, width), BF)] * seats
        + [struct((full, width), F4), struct((full, width), F4), struct((full, width), BF)]
        + [struct((8, width), F4), struct((1, hidden), F4)]
        + grad_shapes(width, hidden + width, fast)
        + grad_shapes(hidden, width, fast)
    )
    result = pl.pallas_call(
        functools.partial(middle_kernel, seats, nparts),
        name="middle",
        in_specs=[smem_spec()] + [any_spec()] * (2 * seats + 3 * nparts) + [whole] * 4,
        out_specs=[any_spec()] * seats + [whole] * 5 + [any_spec()] * (2 * nparts),
        out_shape=out_shape,
        scratch_shapes=[
            pltpu.VMEM((full, width), BF),
            pltpu.VMEM((full, width), BF),
            pltpu.VMEM((width, width), BF),
            pltpu.VMEM((width, hidden), BF),
            pltpu.VMEM((hidden, width), BF),
            pltpu.VMEM((full, width), BF),
            pltpu.VMEM((full, width), BF),
            pltpu.VMEM((full, hidden), BF),
            pltpu.VMEM((full, hidden), BF),
            pltpu.VMEM((full, width), BF),
            pltpu.VMEM((full, width), BF),
            pltpu.VMEM((width, hidden + width), BF),
            pltpu.VMEM((hidden, width), BF),
            pltpu.SemaphoreType.DMA((5,)),
        ],
        compiler_params=params(),
        cost_estimate=cost(20e9, 25e6),
    )(place, x_own, *x_got, g_own, *g_got, *co_parts, *up_parts, *down_parts, cctx, xhat, vec, bias)
    outs, rest = result[:seats], result[seats:]
    return outs, rest[:5], rest[5 : 5 + nparts], rest[5 + nparts :]


def attend_back_kernel(causal, qa, ka, value, ctx, dctx, tri, dq, dk, dv):
    own, spot = lane_masks(F4)
    total = value.shape[0]
    blocks = total // TILE
    upstream = dctx[...].astype(F4)
    product = upstream * ctx[...].astype(F4)
    row = lax.broadcasted_iota(jnp.int32, (PAIR, PAIR), 0) // HEAD
    col = lax.broadcasted_iota(jnp.int32, (PAIR, PAIR), 1) // HEAD
    swap = jnp.where(row != col, -1.0, 0.0).astype(BF)
    high = product.astype(BF)
    delta = mm(high, swap) + mm((product - high.astype(F4)).astype(BF), swap)
    delta_high = delta.astype(BF).astype(F4)
    delta_low = delta - delta_high
    values = value[...].astype(F4)
    d_query, d_key, d_value = [], [], []
    for h in range(2):
        spots = spot(h, 0) + spot(h, 1)
        do = (upstream * own[h] + delta_high * spot(h, 0) + delta_low * spot(h, 1)).astype(BF)
        va = (values * own[h] + spots).astype(BF)
        query, key = qa[h], ka[h]
        query_t = query.T[h * HEAD : (h + 1) * HEAD]
        do_t = do.T[h * HEAD : (h + 1) * HEAD]
        keys, vals, sums = [], [], [None] * blocks
        for j in range(blocks):
            start = j * TILE if causal else 0
            key_j, va_j = key[j * TILE : (j + 1) * TILE], va[j * TILE : (j + 1) * TILE]
            s = mt(query[start:], key_j)
            if causal:
                head = s[:TILE] + tri[...]
                s = jnp.concatenate([head, s[TILE:]], axis=0) if j < blocks - 1 else head
            prob = jnp.exp2(s * LOG2E)
            ds = (prob * mt(do[start:], va_j)).astype(BF)
            vals.append(mm(do_t[:, start:], prob.astype(BF)))
            keys.append(mm(query_t[:, start:], ds))
            back = mm(ds, key_j)
            for i in range(start // TILE, blocks):
                part = back[i * TILE - start : (i + 1) * TILE - start]
                sums[i] = part if sums[i] is None else sums[i] + part
        d_query.append(jnp.concatenate(sums, axis=0))
        d_key.append(jnp.concatenate(keys, axis=1))
        d_value.append(jnp.concatenate(vals, axis=1))
    dq[...] = ((d_query[0] * own[0] + d_query[1] * own[1]) * HEAD ** (-0.5)).astype(BF)
    dk[...] = jnp.concatenate(d_key, axis=0).T.astype(BF)
    dv[...] = jnp.concatenate(d_value, axis=0).T.astype(BF)


def attend_back(causal, qa, ka, value, ctx, dctx, tri):
    full, width = value.shape
    both = pl.BlockSpec((2, full, PAIR), lambda p: (p, 0, 0))
    cols = pl.BlockSpec((full, PAIR), lambda p: (0, p))
    return pl.pallas_call(
        functools.partial(attend_back_kernel, causal),
        name="self_back" if causal else "cross_back",
        grid=(width // PAIR,),
        in_specs=[both, both, cols, cols, cols, pl.BlockSpec((TILE, TILE), lambda p: (0, 0))],
        out_specs=[cols] * 3,
        out_shape=[struct((full, width), BF)] * 3,
        compiler_params=params(),
        cost_estimate=cost(20e9, 10e6),
    )(qa, ka, value, ctx, dctx, tri)


def cross_grads_kernel(seats, nparts, *refs):
    place, mem_own = refs[0], refs[1]
    mem_got = refs[2 : 1 + seats]
    rest = refs[1 + seats :]
    parts, rest = rest[:nparts], rest[nparts:]
    (dq, dk, dv, ctx, xhat, inv, d2, d3, vec), rest = rest[:9], rest[9:]
    outs, rest = rest[:seats], rest[seats:]
    (d13, dctx, vec_o), rest = rest[:3], rest[3:]
    grads, rest = rest[:nparts], rest[nparts:]
    (m_v, w_v, mg_v, f_v, da_v, g_v, sems) = rest
    full, width = m_v.shape
    seat, me = place[0], place[1]
    start_weight(w_v, parts, 0, me, sems.at[0])
    start_rows(m_v, mem_own, mem_got, seat, sems.at[1])
    vec_o[...] = jnp.zeros(vec_o.shape, F4)
    wait_all(w_v, sems.at[0])
    wait_all(m_v, sems.at[1])

    def tile(i, carry):
        rows = pl.ds(pl.multiple_of(i * TILE, TILE), TILE)
        normed = xhat[rows]
        f_v[rows] = (normed * vec[0:1] + vec[3:4]).astype(BF)
        d_first = d2[rows] + mt(dq[rows], w_v[:, width : 2 * width])
        inverse = jnp.concatenate([inv[rows]] * (width // PAIR), axis=1)
        d_one, gain, shift = norm_back(d_first, normed, inverse, vec[0:1])
        d13[rows] = d3[rows] + d_one
        da = d_one.astype(BF)
        da_v[rows] = da
        dctx[rows] = mt(da, w_v[:, :width]).astype(BF)
        vec_o[0:1] += gain
        vec_o[3:4] += shift
        back = mt(dk[rows], w_v[:, 2 * width : 3 * width]) + mt(dv[rows], w_v[:, 3 * width :])
        mg_v[rows] = back.astype(BF)
        return carry

    lax.fori_loop(0, full // TILE, tile, 0)
    start_blocks(mg_v, outs, seat, sems.at[0])
    g_v[:, :width] = tm(ctx[...], da_v[...]).astype(BF)
    g_v[:, width : 2 * width] = tm(f_v[...], dq[...]).astype(BF)
    g_v[:, 2 * width : 3 * width] = tm(m_v[...], dk[...]).astype(BF)
    g_v[:, 3 * width :] = tm(m_v[...], dv[...]).astype(BF)
    start_grad(g_v, grads, me, sems.at[1])
    wait_all(mg_v, sems.at[0])
    wait_all(g_v, sems.at[1])


def cross_grads(place, mem_own, mem_got, parts, dq, dk, dv, ctx, xhat, inv, d2, d3, vec, fast):
    seats, span, width = mem_own.shape
    full = seats * span
    nparts = len(parts)
    whole = pl.BlockSpec(memory_space=pltpu.VMEM)
    result = pl.pallas_call(
        functools.partial(cross_grads_kernel, seats, nparts),
        name="cross_grads",
        in_specs=[smem_spec()] + [any_spec()] * (seats + nparts) + [whole] * 9,
        out_specs=[any_spec()] * seats + [whole] * 3 + [any_spec()] * nparts,
        out_shape=[struct((span, width), BF)] * seats
        + [struct((full, width), F4), struct((full, width), BF), struct((8, width), F4)]
        + grad_shapes(width, 4 * width, fast),
        scratch_shapes=[
            pltpu.VMEM((full, width), BF),
            pltpu.VMEM((width, 4 * width), BF),
            pltpu.VMEM((full, width), BF),
            pltpu.VMEM((full, width), BF),
            pltpu.VMEM((full, width), BF),
            pltpu.VMEM((width, 4 * width), BF),
            pltpu.SemaphoreType.DMA((2,)),
        ],
        compiler_params=params(),
        cost_estimate=cost(5e9, 20e6),
    )(place, mem_own, *mem_got, *parts, dq, dk, dv, ctx, xhat, inv, d2, d3, vec)
    return result[:seats], result[seats : seats + 3], result[seats + 3 :]


def self_grads_kernel(seats, nparts, *refs):
    place, x_own = refs[0], refs[1]
    x_got = refs[2 : 1 + seats]
    rest = refs[1 + seats :]
    parts, rest = rest[:nparts], rest[nparts:]
    (dq, dk, dv, d13), rest = rest[:4], rest[4:]
    outs, rest = rest[:seats], rest[seats:]
    grads, rest = rest[:nparts], rest[nparts:]
    (x_v, w_v, ig_v, g_v, sems) = rest
    full, width = x_v.shape
    seat, me = place[0], place[1]
    start_rows(x_v, x_own, x_got, seat, sems.at[0])
    start_weight(w_v, parts, 0, me, sems.at[1])
    wait_all(x_v, sems.at[0])
    for c, d in enumerate((dq, dk, dv)):
        g_v[:, c * width : (c + 1) * width] = tm(x_v[...], d[...]).astype(BF)
    start_grad(g_v, grads, me, sems.at[0])
    wait_all(w_v, sems.at[1])
    for i in range(0, full, TILE):
        rows = slice(i, i + TILE)
        back = d13[rows]
        for c, d in enumerate((dq, dk, dv)):
            back = back + mt(d[rows], w_v[:, c * width : (c + 1) * width])
        ig_v[rows] = back.astype(BF)
    start_blocks(ig_v, outs, seat, sems.at[1])
    wait_all(g_v, sems.at[0])
    wait_all(ig_v, sems.at[1])


def self_grads(place, x_own, x_got, parts, dq, dk, dv, d13, fast):
    seats, span, width = x_own.shape
    full = seats * span
    nparts = len(parts)
    whole = pl.BlockSpec(memory_space=pltpu.VMEM)
    result = pl.pallas_call(
        functools.partial(self_grads_kernel, seats, nparts),
        name="self_grads",
        in_specs=[smem_spec()] + [any_spec()] * (seats + nparts) + [whole] * 4,
        out_specs=[any_spec()] * (seats + nparts),
        out_shape=[struct((span, width), BF)] * seats + grad_shapes(width, 3 * width, fast),
        scratch_shapes=[
            pltpu.VMEM((full, width), BF),
            pltpu.VMEM((width, 3 * width), BF),
            pltpu.VMEM((full, width), BF),
            pltpu.VMEM((width, 3 * width), BF),
            pltpu.SemaphoreType.DMA((2,)),
        ],
        compiler_params=params(),
        cost_estimate=cost(3.5e9, 12e6),
    )(place, x_own, *x_got, *parts, dq, dk, dv, d13)
    return result[:seats], result[seats:]


def unpack_kernel(place, *refs):
    out = refs[-1]
    for r, block in enumerate(refs[:-1]):
        out[place[0] ^ r] = block[...].astype(out.dtype)


def unpack(place, blocks, dtype):
    span, width = blocks[0].shape
    seats = len(blocks)
    whole = pl.BlockSpec(memory_space=pltpu.VMEM)
    return pl.pallas_call(
        unpack_kernel,
        name="unpack",
        in_specs=[smem_spec()] + [whole] * seats,
        out_specs=whole,
        out_shape=struct((seats, span, width), dtype),
        compiler_params=params(),
        cost_estimate=cost(0, 3e6),
    )(place, *blocks)


def pick_kernel(count, place, *refs):
    sources, outs, sem = refs[:count], refs[count:-1], refs[-1]
    seats = sources[0].shape[0]
    copies = []
    for n, out in enumerate(outs):
        src = sources[n // (seats - 1)].at[place[0] ^ (n % (seats - 1) + 1)]
        copies.append(pltpu.make_async_copy(src, out, sem.at[n]))
    for copy in copies:
        copy.start()
    for copy in copies:
        copy.wait()


def pick(place, *sources):
    seats, span, width = sources[0].shape
    number = len(sources) * (seats - 1)
    outs = pl.pallas_call(
        functools.partial(pick_kernel, len(sources)),
        name="pick",
        in_specs=[smem_spec()] + [any_spec()] * len(sources),
        out_specs=[any_spec()] * number,
        out_shape=[struct((span, width), BF)] * number,
        scratch_shapes=[pltpu.SemaphoreType.DMA((number,))],
        compiler_params=params(),
        cost_estimate=cost(0, 2e6),
    )(place, *sources)
    return [outs[k * (seats - 1) : (k + 1) * (seats - 1)] for k in range(len(sources))]


def swap_seats(blocks, seats):
    return [
        lax.ppermute(block, "seq", [(i, i ^ (r + 1)) for i in range(seats)]) for r, block in enumerate(blocks)
    ]


def swap(value, bits):
    return lax.ppermute(value, AXES, [(i, i ^ bits) for i in range(FAST)])


def gather_chain(shard):
    held = jnp.concatenate([shard] + [swap(shard, z << 3) for z in (1, 2, 3)], axis=0)
    for bits in (2, 4):
        held = jnp.concatenate([held, swap(held, bits)], axis=0)
    return [held, swap(held, 1)]


def reduce_chain(parts):
    keep, send = parts
    total = keep.astype(F4) + swap(send, 1).astype(F4)
    for bits in (4, 2):
        half = total.shape[0] // 2
        total = total[:half] + swap(total[half:].astype(BF), bits).astype(F4)
    span = total.shape[0] // 4
    result = total[:span]
    for z in (1, 2, 3):
        result = result + swap(total[z * span : (z + 1) * span].astype(BF), z << 3).astype(F4)
    return result


def on_device(
    inputs,
    memory,
    seg_ids,
    mem_lengths,
    cotangent,
    qkv_weight,
    self_out_weight,
    cross_q_weight,
    cross_kv_weight,
    cross_out_weight,
    ffn_in_weight,
    ffn_in_bias,
    ffn_out_weight,
    norm_gains,
    shift_vectors,
):
    seats = lax.axis_size("seq")
    devices = lax.axis_size("dp") * seats
    span, width = inputs.shape[1:]
    full = seats * span
    seat = lax.axis_index("seq")
    me = lax.axis_index("dp") * seats + seat
    fast = devices == FAST and qkv_weight.shape[0] % 16 == 0
    place = jnp.stack([seat, me]).astype(jnp.int32)

    x_send = pick(place, inputs)[0]
    x_got = swap_seats(x_send, seats)
    second_group = [self_out_weight, cross_q_weight, cross_kv_weight, cross_out_weight]
    if fast:
        qkv_parts = gather_chain(qkv_weight)
        rows, piece = qkv_weight.shape[0], norm_gains.shape[1]
        bias_piece = ffn_in_bias.shape[0]
        block = jnp.concatenate(
            [
                jnp.pad(norm_gains, ((0, 0), (0, PAIR - piece))),
                jnp.pad(shift_vectors, ((0, 0), (0, PAIR - piece))),
                jnp.pad(ffn_in_bias[None], ((0, rows - 8), (0, PAIR - bias_piece))),
            ],
            axis=0,
        )
        two_parts = gather_chain(jnp.concatenate(second_group + [block], axis=1))
        up_parts = gather_chain(ffn_in_weight)
        down_parts = gather_chain(ffn_out_weight)
        blocks = jnp.concatenate([part[:, 5 * width :].reshape(16, rows * PAIR) for part in two_parts], axis=0)
        order = jnp.asarray([rel(p) for p in range(FAST)], jnp.int32)
        chosen = (order[None, :] ^ me) == jnp.arange(FAST, dtype=jnp.int32)[:, None]
        natural = jnp.dot(chosen.astype(BF), blocks, preferred_element_type=F4).reshape(FAST, rows, PAIR)
        vec = jnp.transpose(natural[:, :8, :piece], (1, 0, 2)).reshape(8, FAST * piece)
        bias = natural[:, 7, :bias_piece].reshape(1, FAST * bias_piece)
    else:
        qkv_parts = [lax.all_gather(qkv_weight, AXES, axis=0, tiled=True)]
        two_parts = [lax.all_gather(jnp.concatenate(second_group, axis=1), AXES, axis=0, tiled=True)]
        up_parts = [lax.all_gather(ffn_in_weight, AXES, axis=0, tiled=True)]
        down_parts = [lax.all_gather(ffn_out_weight, AXES, axis=0, tiled=True)]
        vec = lax.all_gather(jnp.concatenate([norm_gains, shift_vectors], axis=0), AXES, axis=1, tiled=True)
        vec = jnp.pad(vec.astype(F4), ((0, 1), (0, 0)))
        bias = lax.all_gather(ffn_in_bias, AXES, axis=0, tiled=True).astype(F4)[None]
    mem_send, cot_send = pick(place, memory, cotangent)
    mem_got = swap_seats(mem_send, seats)
    cot_got = swap_seats(cot_send, seats)

    segments = lax.dynamic_index_in_dim(seg_ids, seat, 0, keepdims=False)
    ends = jnp.cumsum(lax.dynamic_index_in_dim(mem_lengths, seat, 0, keepdims=False))
    places = jnp.arange(full, dtype=jnp.int32)
    mem_segments = jnp.sum((places[:, None] >= ends[None, :]).astype(jnp.int32), axis=1)
    lane = jnp.arange(PAIR, dtype=jnp.int32)
    half = jnp.arange(2, dtype=jnp.int32)[:, None, None]
    free = (lane // HEAD)[None, None] == 1 - half
    number = (lane % HEAD)[None, None]

    def key_side(ids):
        away = jnp.where(ids[None, :, None] == number, 0.0, AWAY)
        ones = jnp.where(number < 11, 1.0, 0.0)
        return jnp.where(free, jnp.where(number < 8, away, ones), 0.0).astype(BF)

    augq = jnp.where(free & (number < 8) & (segments[None, :, None] == number), 1.0, 0.0).astype(BF)
    augk, augm = key_side(segments), key_side(mem_segments)
    corner = jnp.arange(TILE, dtype=jnp.int32)
    tri = jnp.where(corner[None, :] <= corner[:, None], 0.0, AWAY).astype(F4)

    ctx, qa, ka, value = self_forward(place, inputs, x_got, qkv_parts, augq, augk, tri)
    cctx, cqa, cka, cvalue, xhat, inv = cross_forward(
        place, inputs, x_got, memory, mem_got, two_parts, ctx, vec, augq, augm
    )
    outs, (d3, d2, dcctx, vec_mid, bias_grad), upco_g, down_g = middle(
        place, inputs, x_got, cotangent, cot_got, two_parts, up_parts, down_parts, cctx, xhat, vec, bias, fast
    )
    out_got = swap_seats(outs[1:], seats)
    cdq, cdk, cdv = attend_back(False, cqa, cka, cvalue, cctx, dcctx, tri)
    mem_outs, (d13, dctx, vec_first), two_g = cross_grads(
        place, memory, mem_got, two_parts, cdq, cdk, cdv, ctx, xhat, inv, d2, d3, vec, fast
    )
    mg_got = swap_seats(mem_outs[1:], seats)
    dq, dk, dv = attend_back(True, qa, ka, value, ctx, dctx, tri)
    in_outs, qkv_g = self_grads(place, inputs, x_got, qkv_parts, dq, dk, dv, d13, fast)
    ig_got = swap_seats(in_outs[1:], seats)

    vec_sum = (vec_mid + vec_first)[:7]
    if fast:
        down_sum = reduce_chain(down_g)
        upco_sum = reduce_chain(upco_g)
        two_sum = reduce_chain(two_g)
        small = jnp.concatenate([vec_sum, jnp.zeros((1, width), F4), bias_grad.reshape(-1, width)], axis=0)
        for bits in (1, 2, 4, 8, 16):
            small = small + swap(small, bits)
        mine = lax.dynamic_slice_in_dim(small[:7], me * piece, piece, axis=1)
        bias_mine = lax.dynamic_slice_in_dim(small[8:].reshape(-1), me * bias_piece, bias_piece)
        qkv_sum = reduce_chain(qkv_g)
    else:

        def scatter(value, dim=0):
            return lax.psum_scatter(value.astype(F4), AXES, scatter_dimension=dim, tiled=True)

        down_sum, upco_sum, two_sum, qkv_sum = [scatter(g[0]) for g in (down_g, upco_g, two_g, qkv_g)]
        mine, bias_mine = scatter(vec_sum, 1), scatter(bias_grad[0])
    hidden = ffn_in_weight.shape[1]
    return (
        unpack(place, [outs[0], *out_got], BF),
        unpack(place, [in_outs[0], *ig_got], F4),
        unpack(place, [mem_outs[0], *mg_got], F4),
        qkv_sum,
        two_sum[:, :width],
        two_sum[:, width : 2 * width],
        two_sum[:, 2 * width :],
        upco_sum[:, hidden:],
        upco_sum[:, :hidden],
        bias_mine,
        down_sum,
        mine[:3],
        mine[3:],
    )


def solution(mesh):
    rows = P("dp", "seq", None)
    weight = P(AXES, None)
    vector = P(None, AXES)
    return jax.shard_map(
        on_device,
        mesh=mesh,
        in_specs=(rows, rows, P("dp", None), P("dp", None), rows)
        + (weight,) * 6
        + (P(AXES), weight, vector, vector),
        out_specs=(rows,) * 3 + (weight,) * 6 + (P(AXES), weight, vector, vector),
        check_vma=False,
    )
```

time: 1990 us -> 457 us (0.23)
  waiting for transfers between devices: 886 us -> 110 us
  matrix products: 433 us -> 0.16 us
  blocking collectives: 429 us -> 0 us
  Pallas kernels: 0 us -> 219 us
  local copies, waits for them, and re-layouts: 147 us -> 24.9 us
  starting transfers between devices: 29.8 us -> 83 us
  other arithmetic: 47.3 us -> 13.5 us
    reduce_scatter x5 -> x0, waiting for transfers between devices: 553 us -> none  [the longest x1 140 us: on_device(): lax.psum_scatter(d_down, ('dp', 'seq'), scatter_dimension=0, tiled=True)]
    dot_general x77 -> x1, matrix products: 433 us -> 0.16 us  [on_device(): jnp.dot(chosen.astype(BF), blocks, preferred_element_type=F4)]
    all_gather x5 -> x0, blocking collectives: 256 us -> none  [the longest x1 68.1 us: on_device(): lax.all_gather(norm_gains, ('dp', 'seq'), axis=1, tiled=True)]
    unnamed x17 -> x0, waiting for transfers between devices: 242 us -> none
    pallas_call x0 -> x12, Pallas kernels: none -> 219 us  [the longest x2 75.3 us: pick(): pl.pallas_call(functools.partial(pick_kernel, len(sources)), name='pick',...]
    ppermute x0 -> x71, waiting for transfers between devices: none -> 110 us  [the longest x53 97.3 us: swap(): return lax.ppermute(value, AXES, [(i, i ^ bits) for i in range(FAST)])]
    all_to_all x3 -> x0, blocking collectives: 90.8 us -> none  [the longest x1 43.9 us: on_device(): lax.all_to_all(d_qkv_heads.reshape(row_count, full_len, 3, head_part), 's...]
    ppermute x0 -> x71, starting transfers between devices: none -> 83 us  [the longest x53 70.7 us: swap(): return lax.ppermute(value, AXES, [(i, i ^ bits) for i in range(FAST)])]
  transfers between devices with their start and end apart: 20 -> 71, of which waited for: 11 -> 29; matrix products, arithmetic and copies ran while one was open for 20% -> 6% of each run, Pallas kernels for 0% -> 27%
where the time goes in v1:
time: 457 us; the launch traced here: 452 us
  Pallas kernels  219 us (48%)
  waiting for transfers between devices  110 us (24%)
  starting transfers between devices  83 us (18%)
  local copies, waits for them, and re-layouts  24.9 us (5%)
  other arithmetic  13.5 us (3%)
    ppermute x53, waiting for transfers between devices, swap(): return lax.ppermute(value, AXES, [(i, i ^ bits) for i in range(FAST)])  97.3 us
    pallas_call x2, Pallas kernels, pick(): pl.pallas_call(functools.partial(pick_kernel, len(sources)), name='pick',...  75.3 us
    ppermute x53, starting transfers between devices, swap(): return lax.ppermute(value, AXES, [(i, i ^ bits) for i in range(FAST)])  70.7 us
    pallas_call x2, Pallas kernels, attend_back(): pl.pallas_call(functools.partial(attend_back_kernel, causal), name='self_...  43 us
    pallas_call x1, Pallas kernels, middle(): pl.pallas_call(functools.partial(middle_kernel, seats, nparts), name='mid...  31 us
    pallas_call x1, Pallas kernels, cross_forward(): pl.pallas_call(functools.partial(cross_forward_kernel, seats, len(parts))...  21.7 us
    pallas_call x1, Pallas kernels, self_forward(): pl.pallas_call(functools.partial(self_forward_kernel, seats, len(parts)),...  16.6 us
    pallas_call x1, Pallas kernels, cross_grads(): pl.pallas_call(functools.partial(cross_grads_kernel, seats, nparts), name...  15.7 us
  transfers between devices with their start and end apart: 71, of which 29 were waited for; matrix products, arithmetic and copies ran while one was open for 6% of the time, Pallas kernels for 27%

profile of v1, /device:TPU:0, one launch (start us, length us, event | category | flops | bytes accessed | tf_op | source)
XLA Modules:
  0.0 452.3 jit_solution(10050516015675394979)
XLA Ops:
  7.3 3.0 collective-permute-start.6
  13.4 3.9 collective-permute-start.29
  25.5 25.7 %pick.2 = (bf16[256,512]{1,0:T(8,128)(2,1)}, bf16[256,512]{1,0:T(8,128)(2,1)}, bf16[256,512]{1,0:T(8,128)(2,1)}) custom-call(s32[2]{0:T(128)} %pad_add_fusion.place.refs_0_, bf16[4,256,512]{2,1,0:T(8,128)(2,1)} %refs_1_.11), custom_call_target="tpu_custom_call" | custom-call | bytes 2000000 | tf_op jit(solution)/shard_map/pick/pallas_call | solution.py:681
  51.3 49.6 %pick.3 = (bf16[256,512]{1,0:T(8,128)(2,1)}, bf16[256,512]{1,0:T(8,128)(2,1)}, bf16[256,512]{1,0:T(8,128)(2,1)}, bf16[256,512]{1,0:T(8,128)(2,1)}, bf16[256,512]{1,0:T(8,128)(2,1)}, /*index=5*/bf16[256,512]{1,0:T(8,128)(2,1)}) custom-call(s32[2]{0:T(128)} %pad_add_fusion.place.refs_0_, bf16[4,256,512]{2,1,0:T(8,128)(2,1)} %refs_1_.10, ...), custom_call_target="tpu_custom_call" | custom-call | bytes 2000000 | tf_op jit(solution)/shard_map/pick/pallas_call | solution.py:681
  102.3 3.8 collective-permute-start.20
  109.1 4.9 %collective-permute-start.13 = (bf16[16,2048]{1,0:T(8,128)(2,1)S(1)}, bf16[16,2048]{1,0:T(8,128)(2,1)S(1)}, u32[]{:S(2)}, u32[]{:S(2)}) collective-permute-start(bf16[16,2048]{1,0:T(8,128)(2,1)S(1)} %copy-done.8), channel_id=1, source_target_pairs={{0,16},{1,17},{2,18},{3,19},{4,20},{5,21},{6,22},{7,23},{8,24},{9,... | collective-permute-start | bytes 196616 | tf_op jit(solution)/shard_map/ppermute | solution.py:701
  116.4 4.7 %collective-permute-done.14 = bf16[16,2048]{1,0:T(8,128)(2,1)S(1)} collective-permute-done((bf16[16,2048]{1,0:T(8,128)(2,1)S(1)}, bf16[16,2048]{1,0:T(8,128)(2,1)S(1)}, u32[]{:S(2)}, u32[]{:S(2)}) %collective-permute-start.14) | collective-permute-done | bytes 65568 | tf_op jit(solution)/shard_map/ppermute | solution.py:701
  125.5 3.5 collective-permute-done.30
  131.2 11.2 %collective-permute-done.9 = bf16[64,2688]{1,0:T(8,128)(2,1)S(1)} collective-permute-done((bf16[64,2688]{1,0:T(8,128)(2,1)S(1)}, bf16[64,2688]{1,0:T(8,128)(2,1)S(1)}, u32[]{:S(2)}, u32[]{:S(2)}) %collective-permute-start.9) | collective-permute-done | bytes 344096 | tf_op jit(solution)/shard_map/ppermute | solution.py:701
  147.8 13.1 %collective-permute-done.10 = bf16[128,2688]{1,0:T(8,128)(2,1)S(1)} collective-permute-done((bf16[128,2688]{1,0:T(8,128)(2,1)S(1)}, bf16[128,2688]{1,0:T(8,128)(2,1)S(1)}, u32[]{:S(2)}, u32[]{:S(2)}) %collective-permute-start.10) | collective-permute-done | bytes 688160 | tf_op jit(solution)/shard_map/ppermute | solution.py:701
  162.4 9.1 %collective-permute-done.22 = bf16[512,512]{1,0:T(8,128)(2,1)S(1)} collective-permute-done((bf16[512,512]{1,0:T(8,128)(2,1)S(1)}, bf16[512,512]{1,0:T(8,128)(2,1)S(1)}, u32[]{:S(2)}, u32[]{:S(2)}) %collective-permute-start.22) | collective-permute-done | bytes 524320 | tf_op jit(solution)/shard_map/ppermute | solution.py:701
  171.6 5.6 %collective-permute-done.16 = bf16[128,2048]{1,0:T(8,128)(2,1)S(1)} collective-permute-done((bf16[128,2048]{1,0:T(8,128)(2,1)S(1)}, bf16[128,2048]{1,0:T(8,128)(2,1)S(1)}, u32[]{:S(2)}, u32[]{:S(2)}) %collective-permute-start.16) | collective-permute-done | bytes 524320 | tf_op jit(solution)/shard_map/ppermute | solution.py:701
  181.3 16.6 %self_forward.1 = (bf16[1024,512]{1,0:T(8,128)(2,1)}, bf16[8,1024,128]{2,1,0:T(8,128)(2,1)}, bf16[8,1024,128]{2,1,0:T(8,128)(2,1)}, bf16[1024,512]{1,0:T(8,128)(2,1)}) custom-call(s32[2]{0:T(128)} %pad_add_fusion.place.refs_0_, bf16[4,256,512]{2,1,0:T(8,128)(2,1)} %refs_1_.11, bf16[256,512]{1,0:T(8,128)(2,1)} %collective-permute-done.refs_2_, ...), custom_call_target="tpu_custom_call" | custom-call | flops 11000000512 | bytes 8000000 | tf_op jit(solution)/shard_map/self_forward/pallas_call | solution.py:216
  202.6 21.7 %cross_forward.1 = (bf16[1024,512]{1,0:T(8,128)(2,1)}, bf16[8,1024,128]{2,1,0:T(8,128)(2,1)}, bf16[8,1024,128]{2,1,0:T(8,128)(2,1)}, bf16[1024,512]{1,0:T(8,128)...) custom-call(s32[2]{0:T(128)} %pad_add_fusion.place.refs_0_, bf16[4,256,512]{2,1,0:T(8,128)(2,1)} %refs_1_.11, ...), custom_call_target="tpu_custom_call" | custom-call | flops 15000000512 | bytes 14000000 | tf_op jit(solution)/shard_map/cross_forward/pallas_call | solution.py:289
  225.8 31.0 %middle.1 = (bf16[256,512]{1,0:T(8,128)(2,1)}, bf16[256,512]{1,0:T(8,128)(2,1)}, bf16[256,512]{1,0:T(8,128)(2,1)}, bf16[256,512]{1,0:T(8,128)(2,1)}, f32[1024,51...) custom-call(s32[2]{0:T(128)} %pad_add_fusion.place.refs_0_, ...), custom_call_target="tpu_custom_call" | custom-call | flops 20000000000 | bytes 25000000 | tf_op jit(solution)/shard_map/middle/pallas_call | solution.py:426
  258.7 24.3 %cross_back.1 = (bf16[1024,512]{1,0:T(8,128)(2,1)}, bf16[1024,512]{1,0:T(8,128)(2,1)}, bf16[1024,512]{1,0:T(8,128)(2,1)}) custom-call(bf16[8,1024,128]{2,1,0:T(8,128)(2,1)} %get-tuple-element.85.qa, bf16[8,1024,128]{2,1,0:T(8,128)(2,1)} %get-tuple-element.86.ka, bf16[1024,512]{1,0:T(8,128)(2,1)} %get-tuple-element.87.value, ...), custom_call_target="tpu_custom_call" | custom-call | flops 20000000000 | bytes 10000000 | tf_op jit(solution)/shard_map/cross_back/pallas_call | solution.py:505
  283.0 15.7 %cross_grads.1 = (bf16[256,512]{1,0:T(8,128)(2,1)}, bf16[256,512]{1,0:T(8,128)(2,1)}, bf16[256,512]{1,0:T(8,128)(2,1)}, bf16[256,512]{1,0:T(8,128)(2,1)}, f32[10...) custom-call(s32[2]{0:T(128)} %pad_add_fusion.place.refs_0_, ...), custom_call_target="tpu_custom_call" | custom-call | flops 5000000000 | bytes 20000000 | tf_op jit(solution)/shard_map/cross_grads/pallas_call | solution.py:568
  298.7 18.6 %self_back.1 = (bf16[1024,512]{1,0:T(8,128)(2,1)}, bf16[1024,512]{1,0:T(8,128)(2,1)}, bf16[1024,512]{1,0:T(8,128)(2,1)}) custom-call(bf16[8,1024,128]{2,1,0:T(8,128)(2,1)} %get-tuple-element.82.qa, bf16[8,1024,128]{2,1,0:T(8,128)(2,1)} %get-tuple-element.83.ka, bf16[1024,512]{1,0:T(8,128)(2,1)} %get-tuple-element.84.value, ...), custom_call_target="tpu_custom_call" | custom-call | flops 20000000000 | bytes 10000000 | tf_op jit(solution)/shard_map/self_back/pallas_call | solution.py:505
  317.4 8.5 %self_grads.1 = (bf16[256,512]{1,0:T(8,128)(2,1)}, bf16[256,512]{1,0:T(8,128)(2,1)}, bf16[256,512]{1,0:T(8,128)(2,1)}, bf16[256,512]{1,0:T(8,128)(2,1)}, bf16[25...) custom-call(s32[2]{0:T(128)} %pad_add_fusion.place.refs_0_, bf16[4,256,512]{2,1,0:T(8,128)(2,1)} %refs_1_.11, ...), custom_call_target="tpu_custom_call" | custom-call | flops 3500000000 | bytes 12000000 | tf_op jit(solution)/shard_map/self_grads/pallas_call | solution.py:625
  329.9 11.8 %collective-permute-done.61 = f32[12,512]{1,0:T(8,128)S(1)} collective-permute-done((f32[12,512]{1,0:T(8,128)S(1)}, f32[12,512]{1,0:T(8,128)S(1)}, u32[]{:S(2)}, u32[]{:S(2)}) %collective-permute-start.61) | collective-permute-done | bytes 24608 | tf_op jit(solution)/shard_map/ppermute | solution.py:701
  345.6 5.1 %collective-permute-start.63 = (f32[12,512]{1,0:T(8,128)S(1)}, f32[12,512]{1,0:T(8,128)S(1)}, u32[]{:S(2)}, u32[]{:S(2)}) collective-permute-start(f32[12,512]{1,0:T(8,128)S(1)} %add.168), channel_id=1, source_target_pairs={{0,8},{1,9},{2,10},{3,11},{4,12},{5,13},{6,14},{7,15},{8,0},{9,1},... | collective-permute-start | bytes 73736 | tf_op jit(solution)/shard_map/ppermute | solution.py:701
  352.6 3.6 collective-permute-start.64
  362.1 5.9 %collective-permute-done.37.refs_2_ = bf16[256,512]{1,0:T(8,128)(2,1)} collective-permute-done((bf16[256,512]{1,0:T(8,128)(2,1)}, bf16[256,512]{1,0:T(8,128)(2,1)}, u32[]{:S(2)}, u32[]{:S(2)}) %collective-permute-start.37) | collective-permute-done | bytes 262176 | tf_op jit(solution)/shard_map/ppermute | solution.py:696
  368.1 3.9 collective-permute-done.38.refs_3_
  379.3 2.7 unpack.5
  381.9 2.7 unpack.4
  394.1 4.5 collective-permute-done.44
  410.1 5.1 %collective-permute-done.49 = bf16[128,2048]{1,0:T(8,128)(2,1)S(1)} collective-permute-done((bf16[128,2048]{1,0:T(8,128)(2,1)S(1)}, bf16[128,2048]{1,0:T(8,128)(2,1)S(1)}, u32[]{:S(2)}, u32[]{:S(2)}) %collective-permute-start.49) | collective-permute-done | bytes 524320 | tf_op jit(solution)/shard_map/ppermute | solution.py:701
  419.8 2.9 collective-permute-done.50
  425.8 2.9 collective-permute-done.55
  438.2 3.2 collective-permute-done.56
  441.6 2.9 collective-permute-start.58
  (283 shorter events, 119.1 us)
Async XLA Ops:
  7.3 115.3 %collective-permute-start.6 = (bf16[16,2688]{1,0:T(8,128)(2,1)S(1)}, bf16[16,2688]{1,0:T(8,128)(2,1)S(1)}, u32[]{:S(2)}, u32[]{:S(2)}) collective-permute-start(bf16[16,2688]{1,0:T(8,128)(2,1)S(1)} %get-tuple-element.194), channel_id=1, source_target_pairs={{0,8},{1,9},{2,10},{3,11},{4,12},{5,13},{6,14},{7,15},{8,0},{9,1},... | collective-permute-start | bytes 258056 | tf_op jit(solution)/shard_map/ppermute | solution.py:701
  10.4 112.9 %collective-permute-start.7 = (bf16[16,2688]{1,0:T(8,128)(2,1)S(1)}, bf16[16,2688]{1,0:T(8,128)(2,1)S(1)}, u32[]{:S(2)}, u32[]{:S(2)}) collective-permute-start(bf16[16,2688]{1,0:T(8,128)(2,1)S(1)} %get-tuple-element.194), channel_id=1, source_target_pairs={{0,16},{1,17},{2,18},{3,19},{4,20},{5,21},{6,22},{7,23},{8,24},{9,... | collective-permute-start | bytes 258056 | tf_op jit(solution)/shard_map/ppermute | solution.py:701
  13.0 88.0 %collective-permute-start.27 = (bf16[16,1536]{1,0:T(8,128)(2,1)}, bf16[16,1536]{1,0:T(8,128)(2,1)S(1)}, u32[]{:S(2)}, u32[]{:S(2)}) collective-permute-start(bf16[16,1536]{1,0:T(8,128)(2,1)} %param.21), channel_id=1, source_target_pairs={{0,8},{1,9},{2,10},{3,11},{4,12},{5,13},{6,14},{7,15},{8,0},{9,1},... | collective-permute-start | bytes 147464 | tf_op jit(solution)/shard_map/ppermute | solution.py:701
  13.4 88.3 %collective-permute-start.28 = (bf16[16,1536]{1,0:T(8,128)(2,1)}, bf16[16,1536]{1,0:T(8,128)(2,1)S(1)}, u32[]{:S(2)}, u32[]{:S(2)}) collective-permute-start(bf16[16,1536]{1,0:T(8,128)(2,1)} %param.21), channel_id=1, source_target_pairs={{0,16},{1,17},{2,18},{3,19},{4,20},{5,21},{6,22},{7,23},{8,24},{9,... | collective-permute-start | bytes 147464 | tf_op jit(solution)/shard_map/ppermute | solution.py:701
  13.4 88.8 %collective-permute-start.29 = (bf16[16,1536]{1,0:T(8,128)(2,1)}, bf16[16,1536]{1,0:T(8,128)(2,1)S(1)}, u32[]{:S(2)}, u32[]{:S(2)}) collective-permute-start(bf16[16,1536]{1,0:T(8,128)(2,1)} %param.21), channel_id=1, source_target_pairs={{0,24},{1,25},{2,26},{3,27},{4,28},{5,29},{6,30},{7,31},{8,16},{9,... | collective-permute-start | bytes 147464 | tf_op jit(solution)/shard_map/ppermute | solution.py:701
  116.4 61.9 %collective-permute-start = (bf16[256,512]{1,0:T(8,128)(2,1)}, bf16[256,512]{1,0:T(8,128)(2,1)}, u32[]{:S(2)}, u32[]{:S(2)}) collective-permute-start(bf16[256,512]{1,0:T(8,128)(2,1)} %get-tuple-element.66), channel_id=1, source_target_pairs={{0,1},{1,0},{2,3},{3,2},{4,5},{5,4},{6,7},{7,6},{8,9},{9,8},{10,11... | collective-permute-start | bytes 786440 | tf_op jit(solution)/shard_map/ppermute | solution.py:696
  122.7 21.3 %collective-permute-start.21 = (bf16[256,512]{1,0:T(8,128)(2,1)S(1)}, bf16[256,512]{1,0:T(8,128)(2,1)S(1)}, u32[]{:S(2)}, u32[]{:S(2)}) collective-permute-start(bf16[256,512]{1,0:T(8,128)(2,1)S(1)} %pad_maximum_fusion.2), channel_id=1, source_target_pairs={{0,2},{1,3},{2,0},{3,1},{4,6},{5,7},{6,4},{7,5},{8,10},{9,11},{10,... | collective-permute-start | bytes 786440 | tf_op jit(solution)/shard_map/ppermute | solution.py:701
  123.3 21.3 %collective-permute-start.15 = (bf16[64,2048]{1,0:T(8,128)(2,1)S(1)}, bf16[64,2048]{1,0:T(8,128)(2,1)S(1)}, u32[]{:S(2)}, u32[]{:S(2)}) collective-permute-start(bf16[64,2048]{1,0:T(8,128)(2,1)S(1)} %pad_maximum_fusion.1), channel_id=1, source_target_pairs={{0,2},{1,3},{2,0},{3,1},{4,6},{5,7},{6,4},{7,5},{8,10},{9,11},{10,... | collective-permute-start | bytes 786440 | tf_op jit(solution)/shard_map/ppermute | solution.py:701
  142.4 18.4 %collective-permute-start.10 = (bf16[128,2688]{1,0:T(8,128)(2,1)S(1)}, bf16[128,2688]{1,0:T(8,128)(2,1)S(1)}, u32[]{:S(2)}, u32[]{:S(2)}) collective-permute-start(bf16[128,2688]{1,0:T(8,128)(2,1)S(1)} %get-tuple-element.129), channel_id=1, source_target_pairs={{0,4},{1,5},{2,6},{3,7},{4,0},{5,1},{6,2},{7,3},{8,12},{9,13},{10,... | collective-permute-start | bytes 2064392 | tf_op jit(solution)/shard_map/ppermute | solution.py:701
  144.0 27.5 %collective-permute-start.22 = (bf16[512,512]{1,0:T(8,128)(2,1)S(1)}, bf16[512,512]{1,0:T(8,128)(2,1)S(1)}, u32[]{:S(2)}, u32[]{:S(2)}) collective-permute-start(bf16[512,512]{1,0:T(8,128)(2,1)S(1)} %get-tuple-element.140), channel_id=1, source_target_pairs={{0,4},{1,5},{2,6},{3,7},{4,0},{5,1},{6,2},{7,3},{8,12},{9,13},{10,... | collective-permute-start | bytes 1572872 | tf_op jit(solution)/shard_map/ppermute | solution.py:701
  144.7 32.5 %collective-permute-start.16 = (bf16[128,2048]{1,0:T(8,128)(2,1)S(1)}, bf16[128,2048]{1,0:T(8,128)(2,1)S(1)}, u32[]{:S(2)}, u32[]{:S(2)}) collective-permute-start(bf16[128,2048]{1,0:T(8,128)(2,1)S(1)} %get-tuple-element.142), channel_id=1, source_target_pairs={{0,4},{1,5},{2,6},{3,7},{4,0},{5,1},{6,2},{7,3},{8,12},{9,13},{10,... | collective-permute-start | bytes 1572872 | tf_op jit(solution)/shard_map/ppermute | solution.py:701
  147.0 33.4 %collective-permute-start.32 = (bf16[256,1536]{1,0:T(8,128)(2,1)}, bf16[256,1536]{1,0:T(8,128)(2,1)S(1)}, u32[]{:S(2)}, u32[]{:S(2)}) collective-permute-start(bf16[256,1536]{1,0:T(8,128)(2,1)} %constant_dynamic-update-slice_fusion.51.refs_5_), channel_id=1, source_target_pairs={{0,1},{1,0},{2,3},{3,2},{4,5},{5,4},{6,7},{7,6},{8,9},{9,8},{10,11... | collective-permute-start | bytes 2359304 | tf_op jit(solution)/shard_map/ppermute | solution.py:701
  160.8 18.0 %collective-permute-start.1 = (bf16[256,512]{1,0:T(8,128)(2,1)}, bf16[256,512]{1,0:T(8,128)(2,1)}, u32[]{:S(2)}, u32[]{:S(2)}) collective-permute-start(bf16[256,512]{1,0:T(8,128)(2,1)} %get-tuple-element.67), channel_id=1, source_target_pairs={{0,2},{1,3},{2,0},{3,1},{4,6},{5,7},{6,4},{7,5},{8,10},{9,11},{10,... | collective-permute-start | bytes 786440 | tf_op jit(solution)/shard_map/ppermute | solution.py:696
  177.2 20.8 %collective-permute-start.11 = (bf16[256,2688]{1,0:T(8,128)(2,1)S(1)}, bf16[256,2688]{1,0:T(8,128)(2,1)}, u32[]{:S(2)}, u32[]{:S(2)}) collective-permute-start(bf16[256,2688]{1,0:T(8,128)(2,1)S(1)} %constant_dynamic-update-slice_fusion.14.refs_9_.refs_5_), channel_id=1, source_target_pairs={{0,1},{1,0},{2,3},{3,2},{4,5},{5,4},{6,7},{7,6},{8,9},{9,8},{10,11... | collective-permute-start | bytes 4128776 | tf_op jit(solution)/shard_map/ppermute | solution.py:701
  178.3 23.4 %collective-permute-start.24 = (bf16[256,512]{1,0:T(8,128)(2,1)}, bf16[256,512]{1,0:T(8,128)(2,1)}, u32[]{:S(2)}, u32[]{:S(2)}) collective-permute-start(bf16[256,512]{1,0:T(8,128)(2,1)} %get-tuple-element.72), channel_id=1, source_target_pairs={{0,1},{1,0},{2,3},{3,2},{4,5},{5,4},{6,7},{7,6},{8,9},{9,8},{10,11... | collective-permute-start | bytes 786440 | tf_op jit(solution)/shard_map/ppermute | solution.py:696
  178.9 23.2 %collective-permute-start.25 = (bf16[256,512]{1,0:T(8,128)(2,1)}, bf16[256,512]{1,0:T(8,128)(2,1)}, u32[]{:S(2)}, u32[]{:S(2)}) collective-permute-start(bf16[256,512]{1,0:T(8,128)(2,1)} %get-tuple-element.73), channel_id=1, source_target_pairs={{0,2},{1,3},{2,0},{3,1},{4,6},{5,7},{6,4},{7,5},{8,10},{9,11},{10,... | collective-permute-start | bytes 786440 | tf_op jit(solution)/shard_map/ppermute | solution.py:696
  180.4 21.7 %collective-permute-start.26 = (bf16[256,512]{1,0:T(8,128)(2,1)}, bf16[256,512]{1,0:T(8,128)(2,1)}, u32[]{:S(2)}, u32[]{:S(2)}) collective-permute-start(bf16[256,512]{1,0:T(8,128)(2,1)} %get-tuple-element.74), channel_id=1, source_target_pairs={{0,3},{1,2},{2,1},{3,0},{4,7},{5,6},{6,5},{7,4},{8,11},{9,10},{10,... | collective-permute-start | bytes 786440 | tf_op jit(solution)/shard_map/ppermute | solution.py:696
  180.4 44.5 %collective-permute-start.3 = (bf16[256,512]{1,0:T(8,128)(2,1)}, bf16[256,512]{1,0:T(8,128)(2,1)}, u32[]{:S(2)}, u32[]{:S(2)}) collective-permute-start(bf16[256,512]{1,0:T(8,128)(2,1)} %get-tuple-element.69), channel_id=1, source_target_pairs={{0,1},{1,0},{2,3},{3,2},{4,5},{5,4},{6,7},{7,6},{8,9},{9,8},{10,11... | collective-permute-start | bytes 786440 | tf_op jit(solution)/shard_map/ppermute | solution.py:696
  198.0 27.0 %collective-permute-start.4 = (bf16[256,512]{1,0:T(8,128)(2,1)}, bf16[256,512]{1,0:T(8,128)(2,1)S(1)}, u32[]{:S(2)}, u32[]{:S(2)}) collective-permute-start(bf16[256,512]{1,0:T(8,128)(2,1)} %get-tuple-element.70), channel_id=1, source_target_pairs={{0,2},{1,3},{2,0},{3,1},{4,6},{5,7},{6,4},{7,5},{8,10},{9,11},{10,... | collective-permute-start | bytes 786440 | tf_op jit(solution)/shard_map/ppermute | solution.py:696
  201.7 23.3 %collective-permute-start.5 = (bf16[256,512]{1,0:T(8,128)(2,1)S(1)}, bf16[256,512]{1,0:T(8,128)(2,1)S(1)}, u32[]{:S(2)}, u32[]{:S(2)}) collective-permute-start(bf16[256,512]{1,0:T(8,128)(2,1)S(1)} %copy-done.20), channel_id=1, source_target_pairs={{0,3},{1,2},{2,1},{3,0},{4,7},{5,6},{6,5},{7,4},{8,11},{9,10},{10,... | collective-permute-start | bytes 786440 | tf_op jit(solution)/shard_map/ppermute | solution.py:696
  202.1 22.9 %collective-permute-start.23 = (bf16[1024,512]{1,0:T(8,128)(2,1)S(1)}, bf16[1024,512]{1,0:T(8,128)(2,1)}, u32[]{:S(2)}, u32[]{:S(2)}) collective-permute-start(bf16[1024,512]{1,0:T(8,128)(2,1)S(1)} %copy-done.17), channel_id=1, source_target_pairs={{0,1},{1,0},{2,3},{3,2},{4,5},{5,4},{6,7},{7,6},{8,9},{9,8},{10,11... | collective-permute-start | bytes 3145736 | tf_op jit(solution)/shard_map/ppermute | solution.py:701
  202.1 22.9 %collective-permute-start.17 = (bf16[256,2048]{1,0:T(8,128)(2,1)S(1)}, bf16[256,2048]{1,0:T(8,128)(2,1)}, u32[]{:S(2)}, u32[]{:S(2)}) collective-permute-start(bf16[256,2048]{1,0:T(8,128)(2,1)S(1)} %constant_dynamic-update-slice_fusion.29.refs_11_), channel_id=1, source_target_pairs={{0,1},{1,0},{2,3},{3,2},{4,5},{5,4},{6,7},{7,6},{8,9},{9,8},{10,11... | collective-permute-start | bytes 3145736 | tf_op jit(solution)/shard_map/ppermute | solution.py:701
  325.9 47.2 %collective-permute-start.42 = (bf16[256,1536]{1,0:T(8,128)(2,1)}, bf16[256,1536]{1,0:T(8,128)(2,1)S(1)}, u32[]{:S(2)}, u32[]{:S(2)}) collective-permute-start(bf16[256,1536]{1,0:T(8,128)(2,1)} %get-tuple-element.109), channel_id=1, source_target_pairs={{0,1},{1,0},{2,3},{3,2},{4,5},{5,4},{6,7},{7,6},{8,9},{9,8},{10,11... | collective-permute-start | bytes 2359304 | tf_op jit(solution)/shard_map/ppermute | solution.py:701
  326.6 31.4 %collective-permute-start.39 = (bf16[256,512]{1,0:T(8,128)(2,1)S(1)}, bf16[256,512]{1,0:T(8,128)(2,1)S(1)}, u32[]{:S(2)}, u32[]{:S(2)}) collective-permute-start(bf16[256,512]{1,0:T(8,128)(2,1)S(1)} %copy-done.23), channel_id=1, source_target_pairs={{0,1},{1,0},{2,3},{3,2},{4,5},{5,4},{6,7},{7,6},{8,9},{9,8},{10,11... | collective-permute-start | bytes 786440 | tf_op jit(solution)/shard_map/ppermute | solution.py:696
  326.7 31.9 %collective-permute-start.40 = (bf16[256,512]{1,0:T(8,128)(2,1)S(1)}, bf16[256,512]{1,0:T(8,128)(2,1)}, u32[]{:S(2)}, u32[]{:S(2)}) collective-permute-start(bf16[256,512]{1,0:T(8,128)(2,1)S(1)} %copy-done.22), channel_id=1, source_target_pairs={{0,2},{1,3},{2,0},{3,1},{4,6},{5,7},{6,4},{7,5},{8,10},{9,11},{10,... | collective-permute-start | bytes 786440 | tf_op jit(solution)/shard_map/ppermute | solution.py:696
  328.4 31.4 %collective-permute-start.41 = (bf16[256,512]{1,0:T(8,128)(2,1)S(1)}, bf16[256,512]{1,0:T(8,128)(2,1)}, u32[]{:S(2)}, u32[]{:S(2)}) collective-permute-start(bf16[256,512]{1,0:T(8,128)(2,1)S(1)} %copy-done.21), channel_id=1, source_target_pairs={{0,3},{1,2},{2,1},{3,0},{4,7},{5,6},{6,5},{7,4},{8,11},{9,10},{10,... | collective-permute-start | bytes 786440 | tf_op jit(solution)/shard_map/ppermute | solution.py:696
  358.1 30.7 %collective-permute-start.65 = (bf16[1024,512]{1,0:T(8,128)(2,1)}, bf16[1024,512]{1,0:T(8,128)(2,1)S(1)}, u32[]{:S(2)}, u32[]{:S(2)}) collective-permute-start(bf16[1024,512]{1,0:T(8,128)(2,1)} %get-tuple-element.118), channel_id=1, source_target_pairs={{0,1},{1,0},{2,3},{3,2},{4,5},{5,4},{6,7},{7,6},{8,9},{9,8},{10,11... | collective-permute-start | bytes 3145736 | tf_op jit(solution)/shard_map/ppermute | solution.py:701
  362.0 31.1 %collective-permute-start.48 = (bf16[256,2048]{1,0:T(8,128)(2,1)}, bf16[256,2048]{1,0:T(8,128)(2,1)S(1)}, u32[]{:S(2)}, u32[]{:S(2)}) collective-permute-start(bf16[256,2048]{1,0:T(8,128)(2,1)} %get-tuple-element.111), channel_id=1, source_target_pairs={{0,1},{1,0},{2,3},{3,2},{4,5},{5,4},{6,7},{7,6},{8,9},{9,8},{10,11... | collective-permute-start | bytes 3145736 | tf_op jit(solution)/shard_map/ppermute | solution.py:701
  389.1 19.2 %collective-permute-start.66 = (bf16[512,512]{1,0:T(8,128)(2,1)S(1)}, bf16[512,512]{1,0:T(8,128)(2,1)S(1)}, u32[]{:S(2)}, u32[]{:S(2)}) collective-permute-start(bf16[512,512]{1,0:T(8,128)(2,1)S(1)} %slice.289), channel_id=1, source_target_pairs={{0,4},{1,5},{2,6},{3,7},{4,0},{5,1},{6,2},{7,3},{8,12},{9,13},{10,... | collective-permute-start | bytes 1572872 | tf_op jit(solution)/shard_map/ppermute | solution.py:701
  393.5 21.7 %collective-permute-start.49 = (bf16[128,2048]{1,0:T(8,128)(2,1)S(1)}, bf16[128,2048]{1,0:T(8,128)(2,1)S(1)}, u32[]{:S(2)}, u32[]{:S(2)}) collective-permute-start(bf16[128,2048]{1,0:T(8,128)(2,1)S(1)} %slice.290), channel_id=1, source_target_pairs={{0,4},{1,5},{2,6},{3,7},{4,0},{5,1},{6,2},{7,3},{8,12},{9,13},{10,... | collective-permute-start | bytes 1572872 | tf_op jit(solution)/shard_map/ppermute | solution.py:701
  403.6 25.1 %collective-permute-start.55 = (bf16[128,2560]{1,0:T(8,128)(2,1)S(1)}, bf16[128,2560]{1,0:T(8,128)(2,1)S(1)}, u32[]{:S(2)}, u32[]{:S(2)}) collective-permute-start(bf16[128,2560]{1,0:T(8,128)(2,1)S(1)} %slice.288), channel_id=1, source_target_pairs={{0,4},{1,5},{2,6},{3,7},{4,0},{5,1},{6,2},{7,3},{8,12},{9,13},{10,... | collective-permute-start | bytes 1966088 | tf_op jit(solution)/shard_map/ppermute | solution.py:701
  416.7 18.2 %collective-permute-start.68 = (bf16[64,512]{1,0:T(8,128)(2,1)S(1)}, bf16[64,512]{1,0:T(8,128)(2,1)S(1)}, u32[]{:S(2)}, u32[]{:S(2)}) collective-permute-start(bf16[64,512]{1,0:T(8,128)(2,1)S(1)} %get-tuple-element.134), channel_id=1, source_target_pairs={{0,8},{1,9},{2,10},{3,11},{4,12},{5,13},{6,14},{7,15},{8,0},{9,1},... | collective-permute-start | bytes 196616 | tf_op jit(solution)/shard_map/ppermute | solution.py:701
  (65 other events, 734.2 us)
